TPU v7x, 128 devices: a whole 4x4x4 slice. The times are simulated.
128 devices in a mesh: dp: 4 (over x), pipe: 2 (over z_hi), tensor: 16 (over z_lo, y, core).
Axes of the slice: x: 4, y: 4, z: 4 (z_hi: 2, z_lo: 2; z = z_hi * 2 + z_lo), core: 2. Of those that a mesh axis runs over, the one named last changes fastest.
Arguments:
- activations: bfloat16 [4, 256, 12288], P(None, 'dp', 'tensor'), may hold values from -40 to 40
- gains: float32 [2, 12288], P('pipe', 'tensor'), may hold values from 0.1 to 1.9
- block_values: bfloat16 [2, 192, 48, 4096], P('pipe', 'tensor'), may hold values from -0.109375 to 0.109375
- block_rows: int32 [2, 192, 48], P('pipe', 'tensor'), may hold values from 0 to 191, as said below
Outputs:
- hessians: float32 [2, 12288, 12288], P('pipe', 'dp', 'tensor')
- sections: bfloat16 [2, 4, 256, 12288], P('pipe', None, 'dp', 'tensor')
Inputs may be any that keep to these rules, and one draw needn't show every extreme that they name: `block_rows`: for each section and column block the 48 row-block numbers are distinct.
All inputs are finite; a program needn't handle non-finite values.
Results may differ from a plain program's by a relative error of at most 0.009.
Values may be sent and summed in bfloat16 or wider, within the bound.
No kernel may reach another device: no remote copies, remote signals or barrier semaphores. Data moves between devices by JAX's collectives and lax.ppermute only.
A program may use at most 192 MiB of HBM per device.

v0:
```python
import jax
import jax.numpy as jnp
from jax import lax
from jax.sharding import PartitionSpec as P

D = 12288
BLOCK = 64
M = 4
TOK = 64


epsilon_value = 1e-05


def from_behind(value, axis, steps):
    count = lax.axis_size(axis)
    leading, last = (max(0, -steps), min(count, count - steps))
    return lax.ppermute(value, axis, [(source, source + steps) for source in range(leading, last)])


def build_dense(values, rows_index):
    col_blocks = values.shape[0]
    keep_count = values.shape[1]
    row_blocks = D // BLOCK
    picks = (
        rows_index[:, :, None] == jnp.arange(row_blocks, dtype=jnp.int32)[None, None, :]
    ).astype(jnp.bfloat16)
    tiles = values.reshape(col_blocks, keep_count, BLOCK, BLOCK)
    dense = jnp.einsum("jkr,jkab->rajb", picks, tiles, preferred_element_type=jnp.float32)
    return dense.astype(jnp.bfloat16).reshape(D, col_blocks * BLOCK)


def place(store, item, slot, valid):
    previous = lax.dynamic_index_in_dim(store, slot, 0, keepdims=False)
    return lax.dynamic_update_index_in_dim(store, jnp.where(valid, item, previous), slot, 0)


def body(activations, gains, block_values, block_rows):
    segment_count = lax.axis_size("pipe")
    segment = lax.axis_index("pipe")
    width_local = activations.shape[2]
    gain = gains[0]
    values = block_values[0]
    rows_index = block_rows[0]
    dense_weight = build_dense(values, rows_index)
    received = jnp.zeros((TOK, width_local), jnp.bfloat16)
    stash_all = jnp.zeros((M, TOK, D), jnp.bfloat16)
    out_all = jnp.zeros((M, TOK, width_local), jnp.bfloat16)
    for step in range(M + segment_count - 1):
        own_rows = activations[min(step, M - 1)]
        stream = jnp.where(segment == 0, own_rows, received)
        values_f = stream.astype(jnp.float32)
        totals = lax.psum(
            (jnp.sum(values_f, axis=1), jnp.sum(values_f * values_f, axis=1)), "tensor"
        )
        mean = totals[0] / D
        square = totals[1] / D
        scaled = (values_f - mean[:, None]) * lax.rsqrt(square - mean * mean + epsilon_value)[
            :, None
        ]
        normed = (scaled * gain[None, :]).astype(jnp.bfloat16)
        absorb_piece = lax.all_gather(normed, "tensor", axis=1, tiled=True)
        stash = absorb_piece
        product = jnp.dot(absorb_piece, dense_weight, preferred_element_type=jnp.float32)
        product, stash = (product, stash)
        updated = (values_f + product).astype(jnp.bfloat16)
        micro = step - segment
        valid = (micro >= 0) & (micro < M)
        slot = jnp.clip(micro, 0, M - 1)
        stash_all = place(stash_all, stash, slot, valid)
        out_all = place(out_all, updated, slot, valid)
        received = from_behind(updated, "pipe", 1)
    flat = stash_all.reshape(M * TOK, D)
    first_col = lax.axis_index("tensor") * width_local
    own_cols = lax.dynamic_slice_in_dim(flat, first_col, width_local, 1)
    dp_count = lax.axis_size("dp")
    quarters = lax.all_to_all(flat, "dp", split_axis=1, concat_axis=0, tiled=True)
    gram = lax.dot_general(
        quarters,
        lax.all_gather(own_cols, "dp", axis=0, tiled=True),
        (((0,), (0,)), ((), ())),
        preferred_element_type=jnp.float32,
    )
    hessian = gram * (2.0 / (M * TOK * dp_count))
    return (hessian[None], out_all[None])


def solution(mesh):
    return jax.shard_map(
        body,
        mesh=mesh,
        in_specs=(
            P(None, "dp", "tensor"),
            P("pipe", "tensor"),
            P("pipe", "tensor", None, None),
            P("pipe", "tensor", None),
        ),
        out_specs=(P("pipe", "dp", "tensor"), P("pipe", None, "dp", "tensor")),
        check_vma=False,
    )
```

profile of v0, /device:TPU:1, one launch (start us, length us, event | category | flops | bytes accessed | tf_op | source)
XLA Modules:
  0.0 633.5 jit_solution(1971812944985087294)
XLA Ops:
  7.2 1.0 convert_reduce_fusion.4
  8.2 1.0 fusion.17
  9.3 28.6 %all-reduce.4 = (f32[64]{0:T(128)S(1)}, f32[64]{0:T(128)S(1)}) all-reduce(f32[64]{0:T(128)S(1)} %fusion.17, f32[64]{0:T(128)S(1)} %convert_reduce_fusion.4), channel_id=1, replica_groups=mesh['dp'=4,'pipe'=2,'tensor'=16] {'tensor'}, use_global_device_ids=true, to_apply=%region_3.4 | all-reduce | flops 128 | bytes 1024 | tf_op jit(solution)/shard_map/psum | solution.py:53
  38.6 1.6 fusion.16
  40.3 13.7 %reshape_squeeze.3 = bf16[12,48,64,64]{3,2,1,0:T(8,128)(2,1)} reshape(bf16[1,12,48,4096]{3,2,1,0:T(8,128)(2,1)} %param.6) | data formatting | bytes 9437184 | tf_op jit(solution)/shard_map/reshape;squeeze | solution.py:28
  54.1 16.8 %convert_bitcast_fusion = bf16[192,64,12,64]{0,3,1,2:T(8,128)(2,1)} fusion(bf16[12,48,64,64]{3,2,1,0:T(8,128)(2,1)} %reshape_squeeze.3, s32[12,48]{1,0:T(8,128)S(1)} %bitcast.116), kind=kOutput, calls=%fused_computation | convolution fusion | flops 915517440 | bytes 23595264 | tf_op jit(solution)/shard_map/jkr,jkab->rajb/dot_general | solution.py:29
  70.9 47.9 %copy.13 = bf16[192,64,12,64]{1,0,3,2:T(8,128)(2,1)} copy(bf16[192,64,12,64]{0,3,1,2:T(8,128)(2,1)} %convert_bitcast_fusion) | data formatting | bytes 37748736 | tf_op jit(solution)/shard_map/convert_element_type | solution.py:30
  118.9 48.6 %reshape.32 = bf16[12288,768]{0,1:T(8,128)(2,1)} reshape(bf16[192,64,12,64]{1,0,3,2:T(8,128)(2,1)} %copy.13) | data formatting | bytes 37748736 | tf_op jit(solution)/shard_map/reshape | solution.py:30
  167.5 12.7 %bitcast_dynamic-update-slice_fusion.8 = (bf16[4,64,768]{2,1,0:T(8,128)(2,1)S(1)}, bf16[64,768]{1,0:T(8,128)(2,1)S(1)}) fusion(bf16[4,64,768]{2,1,0:T(8,128)(2,1)S(1)} %broadcast_in_dim.68, s32[]{:T(128)S(6)} %min.16, pred[]{:T(512)S(6)} %and.17, bf16[64,12288]{1,0:T(8,128)(2,1)} %all-gather.7.cloned.1.call-done, bf16[12288,768]{0,1:T(8,128)(2,1)} %reshape.32, ...), kind=kOutput, calls=%fused_computation.70 | convolution fusion | flops 1208205312 | bytes 20742150 | tf_op jit(solution)/shard_map/dot_general | solution.py:64
  180.2 5.2 collective-permute-start
  185.4 1.6 collective-permute-done
  187.2 31.2 %all-reduce.3 = (f32[64]{0:T(128)S(1)}, f32[64]{0:T(128)S(1)}) all-reduce(f32[64]{0:T(128)S(1)} %get-tuple-element.9, f32[64]{0:T(128)S(1)} %get-tuple-element.8), channel_id=1, replica_groups=mesh['dp'=4,'pipe'=2,'tensor'=16] {'tensor'}, use_global_device_ids=true, to_apply=%region_7.8 | all-reduce | flops 128 | bytes 1024 | tf_op jit(solution)/shard_map/psum | solution.py:53
  218.4 0.7 fusion.20
  219.4 33.1 %all-gather.9.cloned.1.call-done = bf16[64,12288]{1,0:T(8,128)(2,1)} async-done(((bf16[64,768]{1,0:T(8,128)(2,1)}), bf16[64,12288]{1,0:T(8,128)(2,1)}) %all-gather.9.cloned.1.call-update) | async-done | bytes 1572880 | tf_op jit(solution)/shard_map/all_gather | solution.py:62
  252.4 12.7 %bitcast_dynamic-update-slice_fusion.7 = (bf16[4,64,768]{2,1,0:T(8,128)(2,1)S(1)}, bf16[64,768]{1,0:T(8,128)(2,1)S(1)}) fusion(bf16[4,64,768]{2,1,0:T(8,128)(2,1)S(1)} %get-tuple-element.34, s32[]{:T(128)S(6)} %min.17, bf16[1,64,768]{2,1,0:T(8,128)(2,1)S(1)} %constant_dynamic-slice_fusion.2, pred[]{:T(512)S(6)} %and.18, ...), kind=kOutput, calls=%fused_computation.68 | convolution fusion | flops 1208156160 | bytes 20840452 | tf_op jit(solution)/shard_map/dot_general | solution.py:64
  265.1 4.6 collective-permute-start.1
  269.8 1.9 collective-permute-done.1
  271.8 27.6 %all-reduce.2 = (f32[64]{0:T(128)S(1)}, f32[64]{0:T(128)S(1)}) all-reduce(f32[64]{0:T(128)S(1)} %get-tuple-element.7, f32[64]{0:T(128)S(1)} %get-tuple-element.6), channel_id=1, replica_groups=mesh['dp'=4,'pipe'=2,'tensor'=16] {'tensor'}, use_global_device_ids=true, to_apply=%region_11.12 | all-reduce | flops 128 | bytes 1024 | tf_op jit(solution)/shard_map/psum | solution.py:53
  299.4 0.7 fusion.24
  301.3 2.7 copy-done
  304.7 29.9 %all-gather.11.cloned.1.call-done = bf16[64,12288]{1,0:T(8,128)(2,1)} async-done(((bf16[64,768]{1,0:T(8,128)(2,1)}), bf16[64,12288]{1,0:T(8,128)(2,1)}) %all-gather.11.cloned.1.call-update) | async-done | bytes 1572880 | tf_op jit(solution)/shard_map/all_gather | solution.py:62
  334.6 13.2 %bitcast_dynamic-update-slice_fusion.6 = (bf16[4,64,768]{2,1,0:T(8,128)(2,1)S(1)}, bf16[64,768]{1,0:T(8,128)(2,1)}) fusion(bf16[4,64,768]{2,1,0:T(8,128)(2,1)S(1)} %get-tuple-element.36, s32[]{:T(128)S(6)} %min.18, bf16[1,64,768]{2,1,0:T(8,128)(2,1)} %constant_dynamic-slice_fusion.1, pred[]{:T(512)S(6)} %and.19, ...), kind=kOutput, calls=%fused_computation.66 | convolution fusion | flops 1208156160 | bytes 20840452 | tf_op jit(solution)/shard_map/dot_general | solution.py:64
  347.9 4.5 collective-permute-start.2
  352.4 1.5 bitcast_dynamic-update-slice_fusion.3
  354.6 1.0 convert_reduce_fusion.1
  355.6 27.6 %all-reduce.1 = (f32[64]{0:T(128)S(1)}, f32[64]{0:T(128)S(1)}) all-reduce(f32[64]{0:T(128)S(1)} %get-tuple-element.5, f32[64]{0:T(128)S(1)} %get-tuple-element.4), channel_id=1, replica_groups=mesh['dp'=4,'pipe'=2,'tensor'=16] {'tensor'}, use_global_device_ids=true, to_apply=%region_15.16 | all-reduce | flops 128 | bytes 1024 | tf_op jit(solution)/shard_map/psum | solution.py:53
  383.2 0.7 fusion.28
  384.2 1.5 constant_dynamic-slice_fusion.6
  385.8 2.9 bitcast_dynamic-update-slice_fusion.2
  388.7 29.6 %all-gather.13.cloned.1.call-done = bf16[64,12288]{1,0:T(8,128)(2,1)} async-done(((bf16[64,768]{1,0:T(8,128)(2,1)}), bf16[64,12288]{1,0:T(8,128)(2,1)}) %all-gather.13.cloned.1.call-update) | async-done | bytes 1572880 | tf_op jit(solution)/shard_map/all_gather | solution.py:62
  418.3 13.4 %bitcast_dynamic-update-slice_fusion.5 = (bf16[4,64,768]{2,1,0:T(8,128)(2,1)S(1)}, bf16[64,768]{1,0:T(8,128)(2,1)}) fusion(bf16[4,64,768]{2,1,0:T(8,128)(2,1)S(1)} %get-tuple-element.38, s32[]{:T(128)S(6)} %min.19, bf16[1,64,768]{2,1,0:T(8,128)(2,1)S(1)} %constant_dynamic-slice_fusion, pred[]{:T(512)S(6)} %and.20, ...), kind=kOutput, calls=%fused_computation.64 | convolution fusion | flops 1208156160 | bytes 20840452 | tf_op jit(solution)/shard_map/dot_general | solution.py:64
  431.7 4.5 collective-permute-start.3
  436.3 1.5 constant_dynamic-slice_fusion.5
  438.5 1.7 convert_reduce_fusion
  440.1 28.1 %all-reduce = (f32[64]{0:T(128)S(1)}, f32[64]{0:T(128)}) all-reduce(f32[64]{0:T(128)S(1)} %get-tuple-element.3, f32[64]{0:T(128)S(1)} %get-tuple-element.2), channel_id=1, replica_groups=mesh['dp'=4,'pipe'=2,'tensor'=16] {'tensor'}, use_global_device_ids=true, to_apply=%region_19.20 | all-reduce | flops 128 | bytes 1024 | tf_op jit(solution)/shard_map/psum | solution.py:53
  468.9 1.6 fusion.32
  470.5 1.5 bitcast_dynamic-update-slice_fusion.1
  472.0 1.5 constant_dynamic-slice_fusion.4
  473.5 31.3 %all-gather.15.cloned.1.call-done = bf16[64,12288]{1,0:T(8,128)(2,1)} async-done(((bf16[64,768]{1,0:T(8,128)(2,1)}), bf16[64,12288]{1,0:T(8,128)(2,1)}) %all-gather.15.cloned.1.call-update) | async-done | bytes 1572880 | tf_op jit(solution)/shard_map/all_gather | solution.py:62
  504.9 1.5 bitcast_dynamic-update-slice_fusion
  506.4 13.4 %all_to_all.14 = bf16[256,4,3072]{2,1,0:T(4,128)(2,1)} reshape(bf16[4,64,12288]{2,1,0:T(8,128)(2,1)} %bitcast_dynamic-update-slice_fusion) | data formatting | bytes 12582912 | tf_op jit(solution)/shard_map/all_to_all | solution.py:77
  519.8 7.3 %copy.14 = bf16[256,4,3072]{2,0,1:T(8,128)(2,1)} copy(bf16[256,4,3072]{2,1,0:T(4,128)(2,1)} %all_to_all.14) | data formatting | bytes 12582912 | tf_op jit(solution)/shard_map/all_to_all | solution.py:77
  527.1 5.4 all-to-all-start
  532.8 1.8 constant_dynamic-slice_fusion.3
  534.6 12.2 %fusion.8 = bf16[1,4,64,768]{3,2,1,0:T(8,128)(2,1)S(1)} fusion(bf16[1,4,64,768]{3,2,1,0:T(8,128)(2,1)S(1)} %copy.30, s32[]{:T(128)S(6)} %min.20, bf16[64,12288]{1,0:T(8,128)(2,1)S(1)} %copy-done.4, bf16[12288,768]{0,1:T(8,128)(2,1)} %reshape.32, bf16[64,768]{1,0:T(8,128)(2,1)S(1)} %copy-done.6, bf16[4,64,768]{2,1,0:T(8,128)(2,1)S(1)} %get-tuple-element.40, ...), kind=kOutput, calls=%fused_computation.24 | convolution fusion | flops 1208156160 | bytes 20742148 | tf_op jit(solution)/shard_map/dot_general | solution.py:64
  546.8 28.9 %all-gather.17.cloned.1.call-done = bf16[1024,768]{1,0:T(8,128)(2,1)} async-done(((bf16[256,768]{1,0:T(8,128)(2,1)}), bf16[1024,768]{1,0:T(8,128)(2,1)}) %all-gather.17.cloned.1.call-update) | async-done | bytes 1572880 | tf_op jit(solution)/shard_map/all_gather | solution.py:80
  575.7 40.6 %all-to-all-done = bf16[256,4,3072]{2,0,1:T(8,128)(2,1)} async-done(((bf16[256,4,3072]{2,0,1:T(8,128)(2,1)}), bf16[256,4,3072]{2,0,1:T(8,128)(2,1)}, u32[]{:S(2)}, u32[]{:S(2)}) %all-to-all-start) | async-done | bytes 6291488 | tf_op jit(solution)/shard_map/all_to_all | solution.py:77
  616.3 9.9 %multiply_bitcast_fusion = f32[1,3072,768]{2,1,0:T(8,128)} fusion(bf16[1024,3072]{1,0:T(8,128)(2,1)} %bitcast.17, bf16[1024,768]{1,0:T(8,128)(2,1)} %all-gather.17.cloned.1.call-done), kind=kOutput, calls=%fused_computation.2 | convolution fusion | flops 4834197504 | bytes 17301504 | tf_op jit(solution)/shard_map/dot_general | solution.py:78
  (51 shorter events, 5.9 us)
Async XLA Ops:
  7.2 160.3 %all-gather.7.cloned.1.call-start = ((), (), s32[]{:S(2)}) async-start(), calls=%async_computation.1 | async-start | bytes 1671168 | tf_op jit(solution)/shard_map/all_gather | solution.py:62
  40.3 212.1 %all-gather.9.cloned.1.call-start = ((), (), s32[]{:S(2)}) async-start(), calls=%async_computation.2 | async-start | bytes 1671168 | tf_op jit(solution)/shard_map/all_gather | solution.py:62
  40.3 13.8 %copy-start.9 = (s32[1,12,48]{2,0,1:T(1,128)S(1)}, s32[1,12,48]{2,0,1:T(1,128)}, u32[]{:S(2)}) copy-start(s32[1,12,48]{2,0,1:T(1,128)} %param.7) | copy-start | bytes 6916
  118.9 48.6 %copy-start.5 = (bf16[4,64,768]{2,1,0:T(8,128)(2,1)S(1)}, bf16[4,64,768]{2,1,0:T(8,128)(2,1)}, u32[]{:S(2)}) copy-start(bf16[4,64,768]{2,1,0:T(8,128)(2,1)} %param.4) | copy-start | bytes 1179652
  180.2 6.8 %collective-permute-start = (bf16[64,768]{1,0:T(8,128)(2,1)S(1)}, bf16[64,768]{1,0:T(8,128)(2,1)S(1)}, u32[]{:S(2)}, u32[]{:S(2)}) collective-permute-start(bf16[64,768]{1,0:T(8,128)(2,1)S(1)} %get-tuple-element.35), channel_id=1, source_target_pairs={{0,16},{1,17},{2,18},{3,19},{4,20},{5,21},{6,22},{7,23},{8,24},{9,... | collective-permute-start | bytes 294920 | tf_op jit(solution)/shard_map/ppermute | solution.py:18
  219.1 115.5 %all-gather.11.cloned.1.call-start = ((), (), s32[]{:S(2)}) async-start(), calls=%async_computation.3 | async-start | bytes 1671168 | tf_op jit(solution)/shard_map/all_gather | solution.py:62
  265.1 35.8 %copy-start.1 = (bf16[64,12288]{1,0:T(8,128)(2,1)S(1)}, bf16[64,12288]{1,0:T(8,128)(2,1)}, u32[]{:S(2)}) copy-start(bf16[64,12288]{1,0:T(8,128)(2,1)} %all-gather.7.cloned.1.call-done) | copy-start | bytes 4718596
  265.1 6.5 %collective-permute-start.1 = (bf16[64,768]{1,0:T(8,128)(2,1)S(1)}, bf16[64,768]{1,0:T(8,128)(2,1)S(1)}, u32[]{:S(2)}, u32[]{:S(2)}) collective-permute-start(bf16[64,768]{1,0:T(8,128)(2,1)S(1)} %get-tuple-element.37), channel_id=1, source_target_pairs={{0,16},{1,17},{2,18},{3,19},{4,20},{5,21},{6,22},{7,23},{8,24},{9,... | collective-permute-start | bytes 294920 | tf_op jit(solution)/shard_map/ppermute | solution.py:18
  271.8 32.3 %copy-start.7 = (bf16[64,768]{1,0:T(8,128)(2,1)}, bf16[64,768]{1,0:T(8,128)(2,1)S(1)}, u32[]{:S(2)}) copy-start(bf16[64,768]{1,0:T(8,128)(2,1)S(1)} %get-tuple-element.22) | copy-start | bytes 294916
  300.2 118.2 %all-gather.13.cloned.1.call-start = ((), (), s32[]{:S(2)}) async-start(), calls=%async_computation.4 | async-start | bytes 1671168 | tf_op jit(solution)/shard_map/all_gather | solution.py:62
  301.3 2.7 copy-start
  304.7 47.6 %copy-start.2 = (bf16[64,12288]{1,0:T(8,128)(2,1)S(1)}, bf16[64,12288]{1,0:T(8,128)(2,1)}, u32[]{:S(2)}) copy-start(bf16[64,12288]{1,0:T(8,128)(2,1)} %all-gather.9.cloned.1.call-done) | copy-start | bytes 4718596
  347.9 6.7 %collective-permute-start.2 = (bf16[64,768]{1,0:T(8,128)(2,1)}, bf16[64,768]{1,0:T(8,128)(2,1)S(1)}, u32[]{:S(2)}, u32[]{:S(2)}) collective-permute-start(bf16[64,768]{1,0:T(8,128)(2,1)} %get-tuple-element.39), channel_id=1, source_target_pairs={{0,16},{1,17},{2,18},{3,19},{4,20},{5,21},{6,22},{7,23},{8,24},{9,... | collective-permute-start | bytes 294920 | tf_op jit(solution)/shard_map/ppermute | solution.py:18
  384.0 120.9 %all-gather.15.cloned.1.call-start = ((), (), s32[]{:S(2)}) async-start(), calls=%async_computation.5 | async-start | bytes 1671168 | tf_op jit(solution)/shard_map/all_gather | solution.py:62
  418.3 52.2 %copy-start.3 = (bf16[64,12288]{1,0:T(8,128)(2,1)S(1)}, bf16[64,12288]{1,0:T(8,128)(2,1)}, u32[]{:S(2)}) copy-start(bf16[64,12288]{1,0:T(8,128)(2,1)} %all-gather.13.cloned.1.call-done) | copy-start | bytes 4718596
  431.7 6.7 %collective-permute-start.3 = (bf16[64,768]{1,0:T(8,128)(2,1)}, bf16[64,768]{1,0:T(8,128)(2,1)S(1)}, u32[]{:S(2)}, u32[]{:S(2)}) collective-permute-start(bf16[64,768]{1,0:T(8,128)(2,1)} %get-tuple-element.41), channel_id=1, source_target_pairs={{0,16},{1,17},{2,18},{3,19},{4,20},{5,21},{6,22},{7,23},{8,24},{9,... | collective-permute-start | bytes 294920 | tf_op jit(solution)/shard_map/ppermute | solution.py:18
  527.1 7.5 %copy-start.4 = (bf16[64,12288]{1,0:T(8,128)(2,1)S(1)}, bf16[64,12288]{1,0:T(8,128)(2,1)}, u32[]{:S(2)}) copy-start(bf16[64,12288]{1,0:T(8,128)(2,1)} %all-gather.15.cloned.1.call-done) | copy-start | bytes 4718596
  527.1 7.5 %copy-start.6 = (bf16[64,768]{1,0:T(8,128)(2,1)S(1)}, bf16[64,768]{1,0:T(8,128)(2,1)}, u32[]{:S(2)}) copy-start(bf16[64,768]{1,0:T(8,128)(2,1)} %get-tuple-element.20) | copy-start | bytes 294916
  527.1 89.2 %all-to-all-start = ((bf16[256,4,3072]{2,0,1:T(8,128)(2,1)}), bf16[256,4,3072]{2,0,1:T(8,128)(2,1)}, u32[]{:S(2)}, u32[]{:S(2)}) async-start(bf16[256,4,3072]{2,0,1:T(8,128)(2,1)} %copy.14), calls=%async_computation | async-start | bytes 12582912 | tf_op jit(solution)/shard_map/all_to_all | solution.py:77
  532.5 43.3 %all-gather.17.cloned.1.call-start = ((), (), s32[]{:S(2)}) async-start(), calls=%async_computation.6 | async-start | bytes 1966080 | tf_op jit(solution)/shard_map/all_gather | solution.py:80
  546.8 79.4 %copy-start.8 = (bf16[1,4,64,768]{3,2,1,0:T(8,128)(2,1)}, bf16[1,4,64,768]{3,2,1,0:T(8,128)(2,1)S(1)}, u32[]{:S(2)}) copy-start(bf16[1,4,64,768]{3,2,1,0:T(8,128)(2,1)S(1)} %fusion.8) | copy-start | bytes 1179652
Sparse Core Ops, SparseCore 0:
  40.4 35.9 all-gather.6
  219.2 33.1 all-gather.8
  300.3 34.2 all-gather.10
  384.1 34.1 all-gather.12
  470.6 34.1 all-gather.14
  534.7 40.9 all-gather.16
where the time goes:
time: 645 us; the launch traced here: 633 us
  waiting for transfers between devices  198 us (31%)
  blocking collectives  143 us (22%)
  local copies, waits for them, and re-layouts  142 us (22%)
  matrix products  90.9 us (14%)
  starting transfers between devices  25.1 us (4%)
  other arithmetic  19.6 us (3%)
  between operations  14.8 us (2%)
    psum x5, blocking collectives, body(): lax.psum((jnp.sum(values_f, axis=1), jnp.sum(values_f * values_f, axis=1)...  143 us
    all_gather x5, waiting for transfers between devices, body(): absorb_piece = lax.all_gather(normed, 'tensor', axis=1, tiled=True)  124 us
    dot_general x5, matrix products, body(): jnp.dot(absorb_piece, dense_weight, preferred_element_type=jnp.float32)  64.2 us
    reshape x1, local copies, waits for them, and re-layouts, build_dense(): return dense.astype(jnp.bfloat16).reshape(D, col_blocks * BLOCK)  48.6 us
    convert_element_type x1, local copies, waits for them, and re-layouts, build_dense(): return dense.astype(jnp.bfloat16).reshape(D, col_blocks * BLOCK)  47.9 us
    all_to_all x1, waiting for transfers between devices, body(): lax.all_to_all(flat, 'dp', split_axis=1, concat_axis=0, tiled=True)  40.6 us
    all_gather x1, waiting for transfers between devices, body(): lax.all_gather(own_cols, 'dp', axis=0, tiled=True)  28.9 us
    all_to_all x2, local copies, waits for them, and re-layouts, body(): lax.all_to_all(flat, 'dp', split_axis=1, concat_axis=0, tiled=True)  20.7 us
  transfers between devices with their start and end apart: 11, of which 10 were waited for; matrix products, arithmetic and copies ran while one was open for 24% of the time, Pallas kernels for 0%

commit v1 on v0

v1 whole, which is shorter than its diff:
```python
import functools

import jax
import jax.numpy as jnp
from jax import lax
from jax.experimental import pallas as pl
from jax.experimental.pallas import tpu as pltpu
from jax.sharding import PartitionSpec as P

D = 12288
BLOCK = 64
KEEP = 48
M = 4
TOK = 64
ROWS = M * TOK
DP = 4
TENSOR = 16
WIDTH = D // TENSOR
QUARTER = D // DP
EPSILON = 1e-05
LANES = 128
VMEM_LIMIT = 56 * 1024 * 1024


def build_kernel(rows_ref, blocks_ref, dense_ref):
    pair = pl.program_id(0)

    @pl.loop(0, D // 256)
    def _(chunk):
        dense_ref[pl.ds(pl.multiple_of(chunk * 256, 256), 256), :] = jnp.zeros((256, LANES), jnp.bfloat16)

    @pl.loop(0, KEEP)
    def _(kept):
        for half in range(2):
            first = pl.multiple_of(rows_ref[2 * pair + half, kept] * BLOCK, BLOCK)
            dense_ref[pl.ds(first, BLOCK), half * BLOCK:(half + 1) * BLOCK] = blocks_ref[half, kept]


def build_dense(values, rows_index):
    col_blocks = values.shape[0]
    blocks = values.reshape(col_blocks, KEEP, BLOCK, BLOCK)
    return pl.pallas_call(
        build_kernel,
        grid_spec=pltpu.PrefetchScalarGridSpec(
            num_scalar_prefetch=1,
            grid=(col_blocks // 2,),
            in_specs=[pl.BlockSpec((2, KEEP, BLOCK, BLOCK), lambda pair, rows: (pair, 0, 0, 0))],
            out_specs=pl.BlockSpec((D, LANES), lambda pair, rows: (0, pair)),
        ),
        out_shape=jax.ShapeDtypeStruct((D, col_blocks * BLOCK), jnp.bfloat16),
        compiler_params=pltpu.CompilerParams(vmem_limit_bytes=VMEM_LIMIT),
        cost_estimate=pl.CostEstimate(flops=0, bytes_accessed=32 * 1024 * 1024, transcendentals=0),
        name="build_dense",
    )(rows_index, blocks)


def layer_kernel(gathered_ref, weight_ref, gains_ref, own_ref, out_ref, stats_ref, rows, weight, total, row_sems, weight_sems):
    def row_copy(block):
        return pltpu.make_async_copy(gathered_ref.at[block], rows.at[block], row_sems.at[block])

    def weight_copy(block):
        span = pl.ds(pl.multiple_of(block * WIDTH, WIDTH), WIDTH)
        return pltpu.make_async_copy(weight_ref.at[span], weight.at[span], weight_sems.at[block])

    @pl.loop(0, TENSOR)
    def _(block):
        row_copy(block).start()

    @pl.loop(0, TENSOR)
    def _(block):
        weight_copy(block).start()

    def sums(block, carry):
        row_copy(block).wait()
        totals, squares = carry
        for part in range(WIDTH // LANES):
            values = rows[block, :, part * LANES:(part + 1) * LANES].astype(jnp.float32)
            totals = totals + values
            squares = squares + values * values
        return totals, squares

    zero = jnp.zeros((ROWS, LANES), jnp.float32)
    totals, squares = lax.fori_loop(0, TENSOR, sums, (zero, zero))
    mean = jnp.sum(totals, axis=1, keepdims=True) / D
    square = jnp.sum(squares, axis=1, keepdims=True) / D
    scale = lax.rsqrt(square - mean * mean + EPSILON)
    lane = lax.broadcasted_iota(jnp.int32, (ROWS, LANES), 1)
    stats_ref[...] = jnp.where(lane == 0, mean, scale)
    total[...] = own_ref[...].astype(jnp.float32)

    @pl.loop(0, TENSOR)
    def _(block):
        centre = stats_ref[:, 0:1]
        factor = stats_ref[:, 1:2]
        values = rows[block].astype(jnp.float32)
        normed = ((values - centre) * factor * gains_ref[pl.ds(block, 1), :]).astype(jnp.bfloat16)
        weight_copy(block).wait()
        span = pl.ds(pl.multiple_of(block * WIDTH, WIDTH), WIDTH)
        total[...] += jnp.dot(normed, weight[span], preferred_element_type=jnp.float32)

    out_ref[...] = total[...].astype(jnp.bfloat16)


def layer(gathered, weight, gains, own):
    vmem = pl.BlockSpec(memory_space=pltpu.VMEM)
    return pl.pallas_call(
        layer_kernel,
        in_specs=[pl.BlockSpec(memory_space=pl.ANY), pl.BlockSpec(memory_space=pl.ANY), vmem, vmem],
        out_specs=[vmem, vmem],
        out_shape=[
            jax.ShapeDtypeStruct((ROWS, WIDTH), jnp.bfloat16),
            jax.ShapeDtypeStruct((ROWS, LANES), jnp.float32),
        ],
        scratch_shapes=[
            pltpu.VMEM((TENSOR, ROWS, WIDTH), jnp.bfloat16),
            pltpu.VMEM((D, WIDTH), jnp.bfloat16),
            pltpu.VMEM((ROWS, WIDTH), jnp.float32),
            pltpu.SemaphoreType.DMA((TENSOR,)),
            pltpu.SemaphoreType.DMA((TENSOR,)),
        ],
        compiler_params=pltpu.CompilerParams(vmem_limit_bytes=VMEM_LIMIT),
        cost_estimate=pl.CostEstimate(flops=2 * ROWS * D * WIDTH, bytes_accessed=2 * D * (WIDTH + ROWS), transcendentals=ROWS),
        name="layer",
    )(gathered, weight, gains, own)


PIECE = 256


def gram_kernel(order_ref, rows_ref, *refs):
    cols_refs, stats_refs = refs[:DP], refs[DP:2 * DP]
    row_gain_ref, col_gain_ref, out_ref, cols = refs[2 * DP:]

    @pl.when((pl.program_id(0) == 0) & (pl.program_id(1) == 0))
    def _():
        for part in range(DP):
            values = cols_refs[part][...].astype(jnp.float32)
            scaled = (values - stats_refs[part][:, 0:1]) * stats_refs[part][:, 1:2]
            cols[part * ROWS:(part + 1) * ROWS, :] = (scaled * col_gain_ref[...]).astype(jnp.bfloat16)

    pieces = []
    for part in range(DP):
        values = rows_ref[order_ref[part], 0].astype(jnp.float32)
        scaled = (values - stats_refs[part][:, 0:1]) * stats_refs[part][:, 1:2]
        pieces.append((scaled * row_gain_ref[0]).astype(jnp.bfloat16))
    left = jnp.concatenate(pieces, axis=0)
    gram = lax.dot_general(left, cols[...], (((0,), (0,)), ((), ())), preferred_element_type=jnp.float32)
    out_ref[...] = gram * (2.0 / (DP * ROWS))


def gram(order, rows, cols, stats, row_gain, col_gain):
    per_block = WIDTH // PIECE
    whole = pl.BlockSpec((1, WIDTH), lambda block, piece, order: (0, 0))
    return pl.pallas_call(
        gram_kernel,
        grid_spec=pltpu.PrefetchScalarGridSpec(
            num_scalar_prefetch=1,
            grid=(DP, per_block),
            in_specs=[pl.BlockSpec((DP, 1, ROWS, PIECE), lambda block, piece, order: (0, block, 0, piece))]
            + [pl.BlockSpec((ROWS, WIDTH), lambda block, piece, order: (0, 0))] * DP
            + [pl.BlockSpec((ROWS, LANES), lambda block, piece, order: (0, 0))] * DP
            + [pl.BlockSpec((1, 1, PIECE), lambda block, piece, order: (block, 0, piece)), whole],
            out_specs=pl.BlockSpec((PIECE, WIDTH), lambda block, piece, order: (block * per_block + piece, 0)),
            scratch_shapes=[pltpu.VMEM((DP * ROWS, WIDTH), jnp.bfloat16)],
        ),
        out_shape=jax.ShapeDtypeStruct((QUARTER, WIDTH), jnp.float32),
        compiler_params=pltpu.CompilerParams(vmem_limit_bytes=VMEM_LIMIT),
        cost_estimate=pl.CostEstimate(
            flops=2 * DP * ROWS * QUARTER * WIDTH, bytes_accessed=4 * QUARTER * WIDTH + 2 * DP * ROWS * (QUARTER + WIDTH), transcendentals=0
        ),
        name="gram",
    )(order, rows, *cols, *stats, row_gain, col_gain)


def turn(value):
    pairs = [
        (d * TENSOR + q * DP + j, q * TENSOR + d * DP + j) for d in range(DP) for q in range(DP) for j in range(TENSOR // DP)
    ]
    return lax.ppermute(value, ("dp", "tensor"), pairs)


def gather_dp(value):
    return [value] + [
        lax.ppermute(value, "dp", [(source, (source + step) % DP) for source in range(DP)]) for step in range(1, DP)
    ]


def body(activations, gains, block_values, block_rows):
    first = lax.axis_index("pipe") == 0
    quarter = lax.axis_index("dp")
    gain = gains[0]
    own = activations.reshape(ROWS, WIDTH)
    with jax.named_scope("rows_first"):
        gathered = lax.all_gather(own, "tensor", axis=0)
    with jax.named_scope("gains"):
        all_gains = lax.all_to_all(jnp.broadcast_to(gain[None, :], (TENSOR, WIDTH)), "tensor", 0, 0, tiled=True)
    with jax.named_scope("weight"):
        weight = build_dense(block_values[0], block_rows[0])
    with jax.named_scope("layer_first"):
        updated_first, stats_first = layer(gathered, weight, all_gains, own)
    with jax.named_scope("hand_over"):
        received = lax.ppermute(updated_first, "pipe", [(0, 1)])
    with jax.named_scope("rows_second"):
        gathered = lax.all_gather(received, "tensor", axis=0)
    with jax.named_scope("hessian_inputs"):
        stream = jnp.where(first, own, received)
        turned = turn(stream)
        hessian_rows = lax.all_gather(turned, "tensor", axis=0)
        cols = gather_dp(stream)
    with jax.named_scope("layer_second"):
        updated_second, stats_second = layer(gathered, weight, all_gains, received)
    with jax.named_scope("hessian"):
        stats = gather_dp(jnp.where(first, stats_first, stats_second))
        row_gain = lax.dynamic_slice_in_dim(all_gains, quarter * (TENSOR // DP), TENSOR // DP, 0)
        order = (quarter - jnp.arange(DP, dtype=jnp.int32)) % DP
        hessian = gram(
            order, hessian_rows.reshape(DP, TENSOR // DP, ROWS, WIDTH), cols, stats, row_gain[:, None, :], gain[None, :]
        )
    sections = jnp.where(first, updated_first, updated_second)
    return (hessian[None], sections.reshape(1, M, TOK, WIDTH))


def solution(mesh):
    return jax.shard_map(
        body,
        mesh=mesh,
        in_specs=(
            P(None, "dp", "tensor"),
            P("pipe", "tensor"),
            P("pipe", "tensor", None, None),
            P("pipe", "tensor", None),
        ),
        out_specs=(P("pipe", "dp", "tensor"), P("pipe", None, "dp", "tensor")),
        check_vma=False,
    )
```

time: 645 us -> 220 us (0.34); the launches traced: 633 us -> 219 us
  blocking collectives: 143 us -> 0 us
  waiting for transfers between devices: 198 us -> 58.5 us
  local copies, waits for them, and re-layouts: 142 us -> 17.8 us
  matrix products: 90.9 us -> 0 us
  Pallas kernels: 0 us -> 80.8 us
  starting transfers between devices: 25.1 us -> 46 us
  other arithmetic: 19.6 us -> 2.18 us
    psum x5 -> x0, blocking collectives: 143 us -> none  [body(): lax.psum((jnp.sum(values_f, axis=1), jnp.sum(values_f * values_f, axis=1)...]
    all_gather x6 -> x3, waiting for transfers between devices: 153 us -> 44.5 us  [the longest x1 23.5 us: body(): gathered = lax.all_gather(received, 'tensor', axis=0)]
    dot_general x7 -> x0, matrix products: 90.9 us -> none  [the longest x5 64.2 us: body(): jnp.dot(absorb_piece, dense_weight, preferred_element_type=jnp.float32)]
    pallas_call x0 -> x4, Pallas kernels: none -> 80.8 us  [the longest x2 33.8 us: layer(): pl.pallas_call(layer_kernel, in_specs=[pl.BlockSpec(memory_space=pl.ANY),...]
    reshape x1 -> x0, local copies, waits for them, and re-layouts: 48.6 us -> none  [build_dense(): return dense.astype(jnp.bfloat16).reshape(D, col_blocks * BLOCK)]
    convert_element_type x1 -> x0, local copies, waits for them, and re-layouts: 47.9 us -> none  [build_dense(): return dense.astype(jnp.bfloat16).reshape(D, col_blocks * BLOCK)]
    all_to_all x1, waiting for transfers between devices: 40.6 us -> 0.01 us  [body(): lax.all_to_all(jnp.broadcast_to(gain[None, :], (TENSOR, WIDTH)), 'tensor'...]
    all_to_all x2 -> x0, local copies, waits for them, and re-layouts: 20.7 us -> none  [body(): lax.all_to_all(flat, 'dp', split_axis=1, concat_axis=0, tiled=True)]
  transfers between devices with their start and end apart: 11 -> 12, of which waited for: 10 -> 6; matrix products, arithmetic and copies ran while one was open for 24% -> 8% of each run, Pallas kernels for 0% -> 21%
where the time goes in v1:
time: 220 us; the launch traced here: 219 us
  Pallas kernels  80.8 us (37%)
  waiting for transfers between devices  58.5 us (27%)
  starting transfers between devices  46 us (21%)
  local copies, waits for them, and re-layouts  17.8 us (8%)
  between operations  13.9 us (6%)
    pallas_call x2, Pallas kernels, layer(): pl.pallas_call(layer_kernel, in_specs=[pl.BlockSpec(memory_space=pl.ANY),...  33.8 us
    ppermute x6, starting transfers between devices, gather_dp(): lax.ppermute(value, 'dp', [(source, (source + step) % DP) for source in r...  32.6 us
    pallas_call x1, Pallas kernels, build_dense(): pl.pallas_call(build_kernel, grid_spec=pltpu.PrefetchScalarGridSpec(num_s...  28.8 us
    all_gather x1, waiting for transfers between devices, body(): gathered = lax.all_gather(received, 'tensor', axis=0)  23.5 us
    all_gather x1, waiting for transfers between devices, body(): hessian_rows = lax.all_gather(turned, 'tensor', axis=0)  20.9 us
    pallas_call x1, Pallas kernels, gram(): pl.pallas_call(gram_kernel, grid_spec=pltpu.PrefetchScalarGridSpec(num_sc...  18.2 us
    squeeze x1, local copies, waits for them, and re-layouts, build_dense(): blocks = values.reshape(col_blocks, KEEP, BLOCK, BLOCK)  13.8 us
    ppermute x1, waiting for transfers between devices, body(): received = lax.ppermute(updated_first, 'pipe', [(0, 1)])  8.74 us
  transfers between devices with their start and end apart: 12, of which 6 were waited for; matrix products, arithmetic and copies ran while one was open for 8% of the time, Pallas kernels for 21%

profile of v1, /device:TPU:1, one launch (start us, length us, event | category | flops | bytes accessed | tf_op | source)
XLA Modules:
  0.0 219.2 jit_solution(3984605309578260046)
XLA Ops:
  7.2 0.0 all-gather.6.cloned.1.call-start
  7.2 0.7 all-gather.6.cloned.1.call-update
  7.9 0.7 reduce
  8.6 0.6 broadcast_in_dim.4
  9.2 7.3 %all-to-all-start = ((f32[16,1,768]{2,1,0:T(1,128)}), f32[16,1,768]{2,1,0:T(1,128)S(1)}, u32[]{:S(2)}, u32[]{:S(2)}) async-start(f32[16,1,768]{2,1,0:T(1,128)} %broadcast_in_dim.4), calls=%async_computation | async-start | bytes 98304 | tf_op jit(solution)/shard_map/gains/all_to_all | solution.py:196
  16.6 0.0 all-gather.10.cloned.1.call-start
  16.6 13.8 %squeeze.7.blocks_ref = bf16[12,48,64,64]{3,2,1,0:T(8,128)(2,1)} reshape(bf16[1,12,48,4096]{3,2,1,0:T(8,128)(2,1)} %param.6) | data formatting | bytes 9437184 | tf_op jit(solution)/shard_map/weight/reshape;weight/squeeze | solution.py:41
  30.4 0.0 copy-done.7
  30.4 0.6 copy.11
  31.0 28.8 %build_dense.1.weight_ref = bf16[12288,768]{1,0:T(8,128)(2,1)} custom-call(s32[12,48]{1,0:T(8,128)} %bitcast.21, bf16[12,48,64,64]{3,2,1,0:T(8,128)(2,1)} %squeeze.7.blocks_ref), custom_call_target="tpu_custom_call" | custom-call | bytes 33554432 | tf_op jit(solution)/shard_map/weight/build_dense/pallas_call | solution.py:42
  59.8 0.0 all-to-all-done
  59.8 0.6 copy.10
  60.4 16.9 %layer.2 = (bf16[256,768]{1,0:T(8,128)(2,1)}, f32[256,128]{1,0:T(8,128)}) custom-call(bf16[16,256,768]{2,1,0:T(8,128)(2,1)} %all-gather.6.cloned.1.call-done.gathered_ref, bf16[12288,768]{1,0:T(8,128)(2,1)} %build_dense.1.weight_ref, f32[16,768]{1,0:T(8,128)} %bitcast.18, bf16[256,768]{1,0:T(8,128)(2,1)} %bitcast.17), custom_call_target="tpu_custom_call" | custom-call | flops 4831838208 | bytes 25165824 | tf_op jit(solution)/shard_map/layer_first/layer/pallas_call | solution.py:106
  77.3 5.3 %collective-permute-start = (bf16[256,768]{1,0:T(8,128)(2,1)}, bf16[256,768]{1,0:T(8,128)(2,1)S(1)}, u32[]{:S(2)}, u32[]{:S(2)}) collective-permute-start(bf16[256,768]{1,0:T(8,128)(2,1)} %get-tuple-element.6), channel_id=1, source_target_pairs={{0,16},{1,17},{2,18},{3,19},{4,20},{5,21},{6,22},{7,23},{8,24},{9,... | collective-permute-start | bytes 1179656 | tf_op jit(solution)/shard_map/hand_over/ppermute | solution.py:202
  82.6 8.7 %collective-permute-done.own_ref = bf16[256,768]{1,0:T(8,128)(2,1)S(1)} collective-permute-done((bf16[256,768]{1,0:T(8,128)(2,1)}, bf16[256,768]{1,0:T(8,128)(2,1)S(1)}, u32[]{:S(2)}, u32[]{:S(2)}) %collective-permute-start) | collective-permute-done | bytes 393248 | tf_op jit(solution)/shard_map/hand_over/ppermute | solution.py:202
  91.3 0.7 copy-done.1
  92.1 0.0 all-gather.10.cloned.1.call-update
  92.1 0.0 all-gather.8.cloned.1.call-start
  92.2 0.0 copy-done
  92.2 0.1 broadcast_select_fusion.1.refs_0_
  92.3 0.0 copy-start.4
  92.3 0.7 collective-permute-start.1
  93.0 0.0 collective-permute-done.1
  93.0 0.0 copy-start.2
  93.0 0.8 copy-done.2
  93.7 0.0 all-gather.8.cloned.1.call-update
  93.8 0.6 and_select_fusion.order_ref
  94.4 0.6 constant_dynamic-slice_fusion.refs_8_
  94.9 16.0 %collective-permute-start.2 = (bf16[256,768]{1,0:T(8,128)(2,1)S(1)}, bf16[256,768]{1,0:T(8,128)(2,1)S(1)}, u32[]{:S(2)}, u32[]{:S(2)}) collective-permute-start(bf16[256,768]{1,0:T(8,128)(2,1)S(1)} %broadcast_select_fusion.1.refs_0_), channel_id=1, source_target_pairs={{0,32},{32,64},{64,96},{96,0},{1,33},{33,65},{65,97},{97,1},{2,34}... | collective-permute-start | bytes 1179656 | tf_op jit(solution)/shard_map/hessian_inputs/ppermute | solution.py:184
  110.9 12.8 %collective-permute-start.3 = (bf16[256,768]{1,0:T(8,128)(2,1)S(1)}, bf16[256,768]{1,0:T(8,128)(2,1)S(1)}, u32[]{:S(2)}, u32[]{:S(2)}) collective-permute-start(bf16[256,768]{1,0:T(8,128)(2,1)S(1)} %broadcast_select_fusion.1.refs_0_), channel_id=1, source_target_pairs={{0,64},{32,96},{64,0},{96,32},{1,65},{33,97},{65,1},{97,33},{2,66}... | collective-permute-start | bytes 1179656 | tf_op jit(solution)/shard_map/hessian_inputs/ppermute | solution.py:184
  123.7 0.0 collective-permute-start.4
  123.7 23.5 %all-gather.10.cloned.1.call-done = bf16[4096,768]{1,0:T(8,128)(2,1)} async-done(((bf16[256,768]{1,0:T(8,128)(2,1)}), bf16[4096,768]{1,0:T(8,128)(2,1)}) %all-gather.10.cloned.1.call-update) | async-done | bytes 6291472 | tf_op jit(solution)/shard_map/rows_second/all_gather | solution.py:204
  147.2 16.9 %layer.3 = (bf16[256,768]{1,0:T(8,128)(2,1)}, f32[256,128]{1,0:T(8,128)}) custom-call(bf16[16,256,768]{2,1,0:T(8,128)(2,1)} %bitcast.15, bf16[12288,768]{1,0:T(8,128)(2,1)} %build_dense.1.weight_ref, f32[16,768]{1,0:T(8,128)} %bitcast.19, bf16[256,768]{1,0:T(8,128)(2,1)} %copy-done.1), custom_call_target="tpu_custom_call" | custom-call | flops 4831838208 | bytes 25165824 | tf_op jit(solution)/shard_map/layer_second/layer/pallas_call | solution.py:106
  164.2 0.0 copy-start.6
  164.2 0.9 collective-permute-start.5
  165.1 1.9 collective-permute-start.6
  166.9 0.0 collective-permute-done.2.refs_1_
  167.0 1.1 collective-permute-start.7
  168.1 0.0 copy-done.3
  168.1 0.8 broadcast_select_fusion
  168.9 0.0 collective-permute-done.3.refs_2_
  168.9 0.0 collective-permute-done.4.refs_3_
  168.9 1.4 collective-permute-done.5.refs_5_
  170.3 2.8 %collective-permute-done.6.refs_6_ = f32[256,128]{1,0:T(8,128)S(1)} collective-permute-done((f32[256,128]{1,0:T(8,128)S(1)}, f32[256,128]{1,0:T(8,128)S(1)}, u32[]{:S(2)}, u32[]{:S(2)}) %collective-permute-start.6) | collective-permute-done | bytes 131104 | tf_op jit(solution)/shard_map/hessian/ppermute | solution.py:184
  173.1 0.3 collective-permute-done.7.refs_7_
  173.5 20.9 %all-gather.8.cloned.1.call-done = bf16[4096,768]{1,0:T(8,128)(2,1)} async-done(((bf16[256,768]{1,0:T(8,128)(2,1)}), bf16[4096,768]{1,0:T(8,128)(2,1)}) %all-gather.8.cloned.1.call-update) | async-done | bytes 6291472 | tf_op jit(solution)/shard_map/hessian_inputs/all_gather | solution.py:208
  194.4 0.0 copy-done.8
  194.5 18.2 %gram.1 = f32[3072,768]{1,0:T(8,128)} custom-call(s32[4]{0:T(128)} %and_select_fusion.order_ref, bf16[4,4,256,768]{3,2,1,0:T(8,128)(2,1)} %bitcast.22, bf16[256,768]{1,0:T(8,128)(2,1)} %copy-done.4, bf16[256,768]{1,0:T(8,128)(2,1)} %copy-done.8, bf16[256,768]{1,0:T(8,128)(2,1)} %copy-done.9, bf16[256,768]{1,0:T(8,128)(2,1)} %copy-done.10, ...), custom_call_target="tpu_custom_call" | custom-call | flops 4831838208 | bytes 17301504 | tf_op jit(solution)/shard_map/hessian/gram/pallas_call | solution.py:154
  (21 shorter events, 0.1 us)
Async XLA Ops:
  7.2 53.3 %all-gather.6.cloned.1.call-start = ((), (), s32[]{:S(2)}) async-start(), calls=%async_computation.1 | async-start | bytes 6684672 | tf_op jit(solution)/shard_map/rows_first/all_gather | solution.py:194
  9.2 50.5 %all-to-all-start = ((f32[16,1,768]{2,1,0:T(1,128)}), f32[16,1,768]{2,1,0:T(1,128)S(1)}, u32[]{:S(2)}, u32[]{:S(2)}) async-start(f32[16,1,768]{2,1,0:T(1,128)} %broadcast_in_dim.4), calls=%async_computation | async-start | bytes 98304 | tf_op jit(solution)/shard_map/gains/all_to_all | solution.py:196
  16.6 13.8 %copy-start.7 = (s32[1,12,48]{2,0,1:T(1,128)S(1)}, s32[1,12,48]{2,0,1:T(1,128)}, u32[]{:S(2)}) copy-start(s32[1,12,48]{2,0,1:T(1,128)} %param.7) | copy-start | bytes 6916
  16.6 130.6 %all-gather.10.cloned.1.call-start = ((), (), s32[]{:S(2)}) async-start(), calls=%async_computation.3 | async-start | bytes 6684672 | tf_op jit(solution)/shard_map/rows_second/all_gather | solution.py:204
  60.4 31.7 %copy-start = (bf16[4,64,768]{2,1,0:T(8,128)(2,1)S(1)}, bf16[4,64,768]{2,1,0:T(8,128)(2,1)}, u32[]{:S(2)}) copy-start(bf16[4,64,768]{2,1,0:T(8,128)(2,1)} %param.4) | copy-start | bytes 1179652
  77.3 14.0 %collective-permute-start = (bf16[256,768]{1,0:T(8,128)(2,1)}, bf16[256,768]{1,0:T(8,128)(2,1)S(1)}, u32[]{:S(2)}, u32[]{:S(2)}) collective-permute-start(bf16[256,768]{1,0:T(8,128)(2,1)} %get-tuple-element.6), channel_id=1, source_target_pairs={{0,16},{1,17},{2,18},{3,19},{4,20},{5,21},{6,22},{7,23},{8,24},{9,... | collective-permute-start | bytes 1179656 | tf_op jit(solution)/shard_map/hand_over/ppermute | solution.py:202
  91.3 0.7 copy-start.1
  92.1 102.3 %all-gather.8.cloned.1.call-start = ((), (), s32[]{:S(2)}) async-start(), calls=%async_computation.2 | async-start | bytes 6684672 | tf_op jit(solution)/shard_map/hessian_inputs/all_gather | solution.py:208
  92.3 102.2 %copy-start.4 = (bf16[256,768]{1,0:T(8,128)(2,1)}, bf16[256,768]{1,0:T(8,128)(2,1)S(1)}, u32[]{:S(2)}) copy-start(bf16[256,768]{1,0:T(8,128)(2,1)S(1)} %broadcast_select_fusion.1.refs_0_) | copy-start | bytes 1179652
  92.3 0.7 collective-permute-start.1
  93.0 0.8 copy-start.2
  94.9 72.0 %collective-permute-start.2 = (bf16[256,768]{1,0:T(8,128)(2,1)S(1)}, bf16[256,768]{1,0:T(8,128)(2,1)S(1)}, u32[]{:S(2)}, u32[]{:S(2)}) collective-permute-start(bf16[256,768]{1,0:T(8,128)(2,1)S(1)} %broadcast_select_fusion.1.refs_0_), channel_id=1, source_target_pairs={{0,32},{32,64},{64,96},{96,0},{1,33},{33,65},{65,97},{97,1},{2,34}... | collective-permute-start | bytes 1179656 | tf_op jit(solution)/shard_map/hessian_inputs/ppermute | solution.py:184
  110.9 57.9 %collective-permute-start.3 = (bf16[256,768]{1,0:T(8,128)(2,1)S(1)}, bf16[256,768]{1,0:T(8,128)(2,1)S(1)}, u32[]{:S(2)}, u32[]{:S(2)}) collective-permute-start(bf16[256,768]{1,0:T(8,128)(2,1)S(1)} %broadcast_select_fusion.1.refs_0_), channel_id=1, source_target_pairs={{0,64},{32,96},{64,0},{96,32},{1,65},{33,97},{65,1},{97,33},{2,66}... | collective-permute-start | bytes 1179656 | tf_op jit(solution)/shard_map/hessian_inputs/ppermute | solution.py:184
  123.7 45.2 %collective-permute-start.4 = (bf16[256,768]{1,0:T(8,128)(2,1)S(1)}, bf16[256,768]{1,0:T(8,128)(2,1)S(1)}, u32[]{:S(2)}, u32[]{:S(2)}) collective-permute-start(bf16[256,768]{1,0:T(8,128)(2,1)S(1)} %broadcast_select_fusion.1.refs_0_), channel_id=1, source_target_pairs={{0,96},{32,0},{64,32},{96,64},{1,97},{33,1},{65,33},{97,65},{2,98}... | collective-permute-start | bytes 1179656 | tf_op jit(solution)/shard_map/hessian_inputs/ppermute | solution.py:184
  147.2 16.9 %copy-start.5 = (f32[256,128]{1,0:T(8,128)S(1)}, f32[256,128]{1,0:T(8,128)}, u32[]{:S(2)}) copy-start(f32[256,128]{1,0:T(8,128)} %get-tuple-element.7) | copy-start | bytes 393220
  147.2 20.8 %copy-start.3 = (bf16[256,768]{1,0:T(8,128)(2,1)S(1)}, bf16[256,768]{1,0:T(8,128)(2,1)}, u32[]{:S(2)}) copy-start(bf16[256,768]{1,0:T(8,128)(2,1)} %get-tuple-element.6) | copy-start | bytes 1179652
  164.2 30.2 %copy-start.6 = (f32[256,128]{1,0:T(8,128)}, f32[256,128]{1,0:T(8,128)S(1)}, u32[]{:S(2)}) copy-start(f32[256,128]{1,0:T(8,128)S(1)} %broadcast_select_fusion.2.refs_4_) | copy-start | bytes 393220
  164.2 6.1 %collective-permute-start.5 = (f32[256,128]{1,0:T(8,128)S(1)}, f32[256,128]{1,0:T(8,128)S(1)}, u32[]{:S(2)}, u32[]{:S(2)}) collective-permute-start(f32[256,128]{1,0:T(8,128)S(1)} %broadcast_select_fusion.2.refs_4_), channel_id=1, source_target_pairs={{0,32},{32,64},{64,96},{96,0},{1,33},{33,65},{65,97},{97,1},{2,34}... | collective-permute-start | bytes 393224 | tf_op jit(solution)/shard_map/hessian/ppermute | solution.py:184
  165.1 8.1 %collective-permute-start.6 = (f32[256,128]{1,0:T(8,128)S(1)}, f32[256,128]{1,0:T(8,128)S(1)}, u32[]{:S(2)}, u32[]{:S(2)}) collective-permute-start(f32[256,128]{1,0:T(8,128)S(1)} %broadcast_select_fusion.2.refs_4_), channel_id=1, source_target_pairs={{0,64},{32,96},{64,0},{96,32},{1,65},{33,97},{65,1},{97,33},{2,66}... | collective-permute-start | bytes 393224 | tf_op jit(solution)/shard_map/hessian/ppermute | solution.py:184
  166.9 27.5 %copy-start.8 = (bf16[256,768]{1,0:T(8,128)(2,1)}, bf16[256,768]{1,0:T(8,128)(2,1)S(1)}, u32[]{:S(2)}) copy-start(bf16[256,768]{1,0:T(8,128)(2,1)S(1)} %collective-permute-done.2.refs_1_) | copy-start | bytes 1179652
  167.0 6.5 %collective-permute-start.7 = (f32[256,128]{1,0:T(8,128)S(1)}, f32[256,128]{1,0:T(8,128)S(1)}, u32[]{:S(2)}, u32[]{:S(2)}) collective-permute-start(f32[256,128]{1,0:T(8,128)S(1)} %broadcast_select_fusion.2.refs_4_), channel_id=1, source_target_pairs={{0,96},{32,0},{64,32},{96,64},{1,97},{33,1},{65,33},{97,65},{2,98}... | collective-permute-start | bytes 393224 | tf_op jit(solution)/shard_map/hessian/ppermute | solution.py:184
  168.9 25.5 %copy-start.9 = (bf16[256,768]{1,0:T(8,128)(2,1)}, bf16[256,768]{1,0:T(8,128)(2,1)S(1)}, u32[]{:S(2)}) copy-start(bf16[256,768]{1,0:T(8,128)(2,1)S(1)} %collective-permute-done.3.refs_2_) | copy-start | bytes 1179652
  168.9 25.5 %copy-start.10 = (bf16[256,768]{1,0:T(8,128)(2,1)}, bf16[256,768]{1,0:T(8,128)(2,1)S(1)}, u32[]{:S(2)}) copy-start(bf16[256,768]{1,0:T(8,128)(2,1)S(1)} %collective-permute-done.4.refs_3_) | copy-start | bytes 1179652
  170.3 24.1 %copy-start.11 = (f32[256,128]{1,0:T(8,128)}, f32[256,128]{1,0:T(8,128)S(1)}, u32[]{:S(2)}) copy-start(f32[256,128]{1,0:T(8,128)S(1)} %collective-permute-done.5.refs_5_) | copy-start | bytes 393220
  173.1 21.3 %copy-start.12 = (f32[256,128]{1,0:T(8,128)}, f32[256,128]{1,0:T(8,128)S(1)}, u32[]{:S(2)}) copy-start(f32[256,128]{1,0:T(8,128)S(1)} %collective-permute-done.6.refs_6_) | copy-start | bytes 393220
  173.5 21.0 %copy-start.13 = (f32[256,128]{1,0:T(8,128)}, f32[256,128]{1,0:T(8,128)S(1)}, u32[]{:S(2)}) copy-start(f32[256,128]{1,0:T(8,128)S(1)} %collective-permute-done.7.refs_7_) | copy-start | bytes 393220
Sparse Core Ops, SparseCore 0:
  9.7 46.1 all-gather.5
  92.2 54.9 all-gather.9
  148.9 45.4 all-gather.7

commit v2 on v1

v2 whole, which is shorter than its diff:
```python
import jax
import jax.numpy as jnp
from jax import lax
from jax.experimental import pallas as pl
from jax.experimental.pallas import tpu as pltpu
from jax.sharding import PartitionSpec as P

D = 12288
BLOCK = 64
KEEP = 48
M = 4
TOK = 64
ROWS = M * TOK
DP = 4
TENSOR = 16
WIDTH = D // TENSOR
QUARTER = D // DP
EPSILON = 1e-05
LANES = 128
SPAN = 256
CHUNK = 64
MIB = 1024 * 1024
VMEM_LIMIT = 61 * MIB
NEAR = [(dz, dy) for dz in range(2) for dy in range(4)]
ANY = pl.BlockSpec(memory_space=pl.ANY)
VMEM = pl.BlockSpec(memory_space=pltpu.VMEM)
SMEM = pl.BlockSpec(memory_space=pltpu.SMEM)


def build_kernel(rows_ref, blocks_ref, dense_ref):
    group = pl.program_id(0)

    @pl.loop(0, D // SPAN)
    def _(chunk):
        dense_ref[0, pl.ds(pl.multiple_of(chunk * SPAN, SPAN), SPAN), :] = jnp.zeros((SPAN, SPAN), jnp.bfloat16)

    per = SPAN // BLOCK

    @pl.loop(0, KEEP, unroll=4)
    def _(kept):
        for part in range(per):
            first = pl.multiple_of(rows_ref[per * group + part, kept] * BLOCK, BLOCK)
            dense_ref[0, pl.ds(first, BLOCK), part * BLOCK:(part + 1) * BLOCK] = blocks_ref[part, kept]


def build_dense(values, rows_index):
    blocks = values.reshape(WIDTH // BLOCK, KEEP, BLOCK, BLOCK)
    per = SPAN // BLOCK
    return pl.pallas_call(
        build_kernel,
        grid_spec=pltpu.PrefetchScalarGridSpec(
            num_scalar_prefetch=1,
            grid=(WIDTH // SPAN,),
            in_specs=[pl.BlockSpec((per, KEEP, BLOCK, BLOCK), lambda group, rows: (group, 0, 0, 0))],
            out_specs=pl.BlockSpec((1, D, SPAN), lambda group, rows: (group, 0, 0)),
        ),
        out_shape=jax.ShapeDtypeStruct((WIDTH // SPAN, D, SPAN), jnp.bfloat16),
        compiler_params=pltpu.CompilerParams(vmem_limit_bytes=VMEM_LIMIT),
        cost_estimate=pl.CostEstimate(flops=0, bytes_accessed=32 * MIB, transcendentals=0),
        name="build_dense",
    )(rows_index, blocks)


def start_pieces(pieces, refs, rows, sems):
    for array, start, count, position, into in pieces:
        pltpu.make_async_copy(
            refs[array].at[pl.ds(start, count)], rows.at[position, pl.ds(into, count)], sems.at[position]
        ).start()


def wait_block(rows, sems, position):
    pltpu.make_async_copy(rows.at[position], rows.at[position], sems.at[position]).wait()


def spread(column, means, span):
    means[span] = jnp.broadcast_to(column, (ROWS, LANES))


def block_at(spot_ref, position):
    side, (dz, dy) = position // len(NEAR), NEAR[position % len(NEAR)]
    z, y, core = (lax.rem(spot_ref[1 + axis] + step, size) for axis, (step, size) in enumerate([(dz, 2), (dy, 4), (side, 2)]))
    return z * 8 + y * 2 + core


def layer_kernel(pieces, count, straight, spot_ref, weight_ref, gains_ref, own_ref, *refs):
    sources, (out_ref, stats_ref, rows, weight, total, means, scales, sems, weight_sems) = refs[:count], refs[count:]

    def place(position):
        return position if straight else block_at(spot_ref, position)

    def weight_copy(position):
        span = pl.ds(pl.multiple_of(place(position) * WIDTH, WIDTH), WIDTH)
        into = pl.ds(position * WIDTH, WIDTH)
        return pltpu.make_async_copy(weight_ref.at[:, span], weight.at[:, into], weight_sems.at[position])

    start_pieces(pieces, sources, rows, sems)
    means[...] = jnp.zeros_like(means)
    scales[...] = jnp.zeros_like(scales)
    total[...] = own_ref[...].astype(jnp.float32)
    for position in range(TENSOR):
        wait_block(rows, sems, position)
        for chunk in range(0, ROWS, CHUNK):
            span = slice(chunk, chunk + CHUNK)
            added = jnp.zeros((CHUNK, LANES), jnp.float32)
            squared = added
            for part in range(WIDTH // LANES):
                values = rows[position, span, part * LANES:(part + 1) * LANES].astype(jnp.float32)
                added = added + values
                squared = squared + values * values
            means[span] += added
            scales[span] += squared
        if position % 2:
            weight_copy(position // 2).start()
    mean = jnp.sum(means[...], axis=1, keepdims=True) / D
    square = jnp.sum(scales[...], axis=1, keepdims=True) / D
    scale = lax.rsqrt(square - mean * mean + EPSILON)
    lane = lax.broadcasted_iota(jnp.int32, (ROWS, LANES), 1)
    stats_ref[...] = jnp.where(lane == 0, mean, scale)
    spread(mean, means, slice(0, ROWS))
    spread(scale, scales, slice(0, ROWS))

    def normalise(position):
        gain = gains_ref[place(position)]
        for chunk in range(0, ROWS, CHUNK):
            span = slice(chunk, chunk + CHUNK)
            for part in range(WIDTH // LANES):
                lanes = slice(part * LANES, (part + 1) * LANES)
                values = rows[position, span, lanes].astype(jnp.float32)
                scaled = (values - means[span]) * scales[span] * gain[:, lanes]
                rows[position, span, lanes] = scaled.astype(jnp.bfloat16)

    normalise(0)
    normalise(1)
    for position in range(0, TENSOR, 2):
        left = jnp.concatenate([rows[position], rows[position + 1]], axis=1)
        for later in range(position + TENSOR // 2, min(position + TENSOR // 2 + 2, TENSOR)):
            weight_copy(later).start()
        weight_copy(position).wait()
        weight_copy(position + 1).wait()
        for group in range(WIDTH // SPAN):
            lanes = slice(group * SPAN, (group + 1) * SPAN)
            right = weight[group, position * WIDTH:(position + 2) * WIDTH]
            total[:, lanes] += jnp.dot(left, right, preferred_element_type=jnp.float32)
        if position + 2 < TENSOR:
            normalise(position + 2)
            normalise(position + 3)
    out_ref[...] = total[...].astype(jnp.bfloat16)


def in_hbm(arrays):
    return [pltpu.with_memory_space_constraint(array, pltpu.HBM) for array in arrays]


def layer(spot, gathered, pieces, weight, gains, own, straight):
    count = len(gathered)
    return pl.pallas_call(
        lambda *refs: layer_kernel(pieces, count, straight, *refs),
        in_specs=[SMEM, ANY, VMEM, VMEM] + [ANY] * count,
        out_specs=[VMEM, VMEM],
        out_shape=[
            jax.ShapeDtypeStruct((ROWS, WIDTH), jnp.bfloat16),
            jax.ShapeDtypeStruct((ROWS, LANES), jnp.float32),
        ],
        scratch_shapes=[
            pltpu.VMEM((TENSOR, ROWS, WIDTH), jnp.bfloat16),
            pltpu.VMEM((WIDTH // SPAN, D, SPAN), jnp.bfloat16),
            pltpu.VMEM((ROWS, WIDTH), jnp.float32),
            pltpu.VMEM((ROWS, LANES), jnp.float32),
            pltpu.VMEM((ROWS, LANES), jnp.float32),
            pltpu.SemaphoreType.DMA((TENSOR,)),
            pltpu.SemaphoreType.DMA((TENSOR,)),
        ],
        compiler_params=pltpu.CompilerParams(vmem_limit_bytes=VMEM_LIMIT),
        cost_estimate=pl.CostEstimate(flops=2 * ROWS * D * WIDTH, bytes_accessed=2 * D * (WIDTH + ROWS), transcendentals=ROWS),
        name="layer",
    )(spot, *in_hbm([weight]), gains, own, *in_hbm(gathered))


PIECE = 384
PER = WIDTH // PIECE
STEPS = QUARTER // PIECE
HALF = TENSOR // DP // 2
CLASSES = [(side, half) for side in range(2) for half in range(HALF)]


def pick_kernel(pieces, count, spot_ref, *refs):
    sources, picked, sems = refs[:count], refs[count:-1], refs[-1]
    for step in range(DP):
        target = lax.rem(spot_ref[0] + step, DP)
        for half in range(HALF):
            dz = lax.rem(target // 2 + 2 - spot_ref[1], 2)
            dy = lax.rem(lax.rem(target, 2) * 2 + half + 4 - spot_ref[2], 4)
            for position in range(len(NEAR)):

                @pl.when(dz * 4 + dy == position)
                def _():
                    for array, start, size, at, row in pieces:
                        if at == position:
                            pltpu.make_async_copy(
                                sources[array].at[pl.ds(start, size)],
                                picked[step].at[pl.ds(half * ROWS + row, size)],
                                sems.at[step, half],
                            ).start()

    for step in range(DP):
        for half in range(HALF):
            block = picked[step].at[pl.ds(half * ROWS, ROWS)]
            pltpu.make_async_copy(block, block, sems.at[step, half]).wait()


def pick(spot, gathered, pieces):
    count = len(gathered)
    return pl.pallas_call(
        lambda *refs: pick_kernel(pieces, count, *refs),
        in_specs=[SMEM] + [ANY] * count,
        out_specs=[VMEM] * DP,
        out_shape=[jax.ShapeDtypeStruct((HALF * ROWS, WIDTH), jnp.bfloat16)] * DP,
        scratch_shapes=[pltpu.SemaphoreType.DMA((DP, HALF))],
        compiler_params=pltpu.CompilerParams(vmem_limit_bytes=VMEM_LIMIT),
        cost_estimate=pl.CostEstimate(flops=0, bytes_accessed=4 * DP * HALF * ROWS * WIDTH, transcendentals=0),
        name="pick",
    )(spot, *in_hbm(gathered))


def after(values, others):
    count = len(values)
    return pl.pallas_call(
        lambda *refs: None,
        in_specs=[ANY] * (count + len(others)),
        out_specs=[ANY] * count,
        out_shape=[jax.ShapeDtypeStruct(value.shape, value.dtype) for value in values],
        input_output_aliases={place: place for place in range(count)},
        name="after",
    )(*in_hbm(values), *others)


def gram_kernel(spot_ref, *refs):
    sources, stats_refs, refs = refs[:2 * DP], refs[2 * DP:3 * DP], refs[3 * DP:]
    cols_ref, row_gain_ref, col_gain_ref, out_ref, rows, cols, means, scales, left, result, sems, row_sems = refs

    def block_of(group):
        side, half = CLASSES[group]
        return lax.rem(spot_ref[3] + side, 2) + 2 * half

    def row_copies(group):
        side, half = CLASSES[group]
        return [
            pltpu.make_async_copy(
                sources[side * DP + part].at[pl.ds(half * ROWS, ROWS)], rows.at[group, part], row_sems.at[group, part]
            )
            for part in range(DP)
        ]

    for group in range(len(CLASSES)):
        for copy in row_copies(group):
            copy.start()
    for part in range(DP):
        spread(stats_refs[part][:, 0:1], means, slice(part * ROWS, (part + 1) * ROWS))
        spread(stats_refs[part][:, 1:2], scales, slice(part * ROWS, (part + 1) * ROWS))
        for chunk in range(0, ROWS, CHUNK):
            span = slice(part * ROWS + chunk, part * ROWS + chunk + CHUNK)
            for lane in range(WIDTH // LANES):
                lanes = slice(lane * LANES, (lane + 1) * LANES)
                values = cols_ref[lax.rem(spot_ref[0] + DP - part, DP), chunk:chunk + CHUNK, lanes].astype(jnp.float32)
                scaled = (values - means[span]) * scales[span] * col_gain_ref[:, lanes]
                cols[span, lanes] = scaled.astype(jnp.bfloat16)

    def normalise(step):
        group, base = step // PER, step % PER * PIECE
        if base == 0:
            for copy in row_copies(group):
                copy.wait()
        gain = row_gain_ref[block_of(group)]
        for part in range(DP):
            for chunk in range(0, ROWS, CHUNK):
                span = slice(part * ROWS + chunk, part * ROWS + chunk + CHUNK)
                for lane in range(PIECE // LANES):
                    from_lanes = slice(base + lane * LANES, base + (lane + 1) * LANES)
                    values = rows[group, part, chunk:chunk + CHUNK, from_lanes].astype(jnp.float32)
                    scaled = (values - means[span]) * scales[span] * gain[:, from_lanes]
                    left[step % 2, span, lane * LANES:(lane + 1) * LANES] = scaled.astype(jnp.bfloat16)

    def store(step):
        row = pl.multiple_of(block_of(step // PER) * WIDTH + step % PER * PIECE, PIECE)
        return pltpu.make_async_copy(result.at[step % 2], out_ref.at[pl.ds(row, PIECE)], sems.at[step % 2])

    normalise(0)
    for step in range(STEPS):
        product = lax.dot_general(
            left[step % 2], cols[...], (((0,), (0,)), ((), ())), preferred_element_type=jnp.float32
        )
        if step >= 2:
            store(step - 2).wait()
        result[step % 2] = product * (2.0 / (DP * ROWS))
        store(step).start()
        if step + 1 < STEPS:
            normalise(step + 1)
    store(STEPS - 2).wait()
    store(STEPS - 1).wait()


def gram(spot, rows, cols, stats, row_gain, col_gain):
    return pl.pallas_call(
        gram_kernel,
        in_specs=[SMEM] + [ANY] * (2 * DP) + [VMEM] * (DP + 3),
        out_specs=ANY,
        out_shape=jax.ShapeDtypeStruct((QUARTER, WIDTH), jnp.float32),
        scratch_shapes=[
            pltpu.VMEM((len(CLASSES), DP, ROWS, WIDTH), jnp.bfloat16),
            pltpu.VMEM((DP * ROWS, WIDTH), jnp.bfloat16),
            pltpu.VMEM((DP * ROWS, LANES), jnp.float32),
            pltpu.VMEM((DP * ROWS, LANES), jnp.float32),
            pltpu.VMEM((2, DP * ROWS, PIECE), jnp.bfloat16),
            pltpu.VMEM((2, PIECE, WIDTH), jnp.float32),
            pltpu.SemaphoreType.DMA((2,)),
            pltpu.SemaphoreType.DMA((len(CLASSES), DP)),
        ],
        compiler_params=pltpu.CompilerParams(vmem_limit_bytes=VMEM_LIMIT),
        cost_estimate=pl.CostEstimate(
            flops=2 * DP * ROWS * QUARTER * WIDTH, bytes_accessed=4 * QUARTER * WIDTH + 2 * DP * ROWS * (QUARTER + WIDTH), transcendentals=0
        ),
        name="gram",
    )(spot, *rows, *stats, cols, row_gain, col_gain)


def along_dp(value, step):
    return lax.ppermute(value, "dp", [(source, (source + step) % DP) for source in range(DP)])


def gather_dp(value):
    return [value] + [along_dp(value, step) for step in range(1, DP)]


def tensor_at(z, y, core):
    return (z % 2) * 8 + (y % 4) * 2 + core % 2


def shift(value, z, y, core):
    pairs = [
        (tensor_at(a, b, c), tensor_at(a + z, b + y, c + core)) for a in range(2) for b in range(4) for c in range(2)
    ]
    return lax.ppermute(value, "tensor", pairs)


def gather_near(value):
    rows = value.shape[0]
    cut, cut2 = rows * 3 // 8, rows * 11 // 16
    up, down, over = shift(value, 0, 1, 0), shift(value, 0, -1, 0), shift(value, 1, 0, 0)
    up2, over_up, over_down = shift(up, 0, 1, 0), shift(up, 1, 0, 0), shift(over, 0, -1, 0)
    far = [
        shift(up2[:cut], 1, 0, 0),
        shift(over_up[cut:cut2], 0, 1, 0),
        shift(over_down[cut2:], 0, -1, 0),
    ]
    mine = [value, down, up2, up, over, over_down, over_up] + far
    theirs = [shift(array, 0, 0, 1) for array in mine]
    pieces = []
    for side in range(2):
        at, pos = side * len(mine), side * len(NEAR)
        pieces += [(at + array, 0, rows, pos + position, 0) for array, position in enumerate([0, 1, 2, 3, 4, 5, 7])]
        pieces += [
            (at + 7, 0, cut, pos + 6, 0),
            (at + 8, 0, cut2 - cut, pos + 6, cut),
            (at + 9, 0, rows - cut2, pos + 6, cut2),
        ]
    return mine + theirs, pieces


def body(activations, gains, block_values, block_rows):
    first = lax.axis_index("pipe") == 0
    quarter = lax.axis_index("dp")
    here = lax.axis_index("tensor")
    gain = gains[0]
    own = activations.reshape(ROWS, WIDTH)
    with jax.named_scope("rows_first"):
        gathered = lax.all_gather(own, "tensor", axis=0, tiled=True)
    with jax.named_scope("gains"):
        all_gains = lax.all_to_all(jnp.broadcast_to(gain[None, :], (TENSOR, WIDTH)), "tensor", 0, 0, tiled=True)
        all_gains = all_gains[:, None, :]
    with jax.named_scope("weight"):
        weight = build_dense(block_values[0], block_rows[0])
    spot = jnp.stack([quarter, here // 8, here // 2 % 4, here % 2]).astype(jnp.int32)
    with jax.named_scope("layer_first"):
        pieces = [(0, block * ROWS, ROWS, block, 0) for block in range(TENSOR)]
        updated_first, _ = layer(spot, [gathered], pieces, weight, all_gains, own, True)
    with jax.named_scope("hand_over"):
        received = lax.ppermute(updated_first, "pipe", [(0, 1)])
    stream = jnp.where(first, own, received)
    with jax.named_scope("columns"):
        cols = lax.all_gather(jnp.where(first, own, 0) + received, "dp", axis=0)
    with jax.named_scope("rows_second"):
        arrays, pieces = gather_near(stream)
    with jax.named_scope("hessian_rows"):
        mine = len(arrays) // 2
        picked = pick(spot, arrays[:mine], [piece for piece in pieces if piece[0] < mine])
        rows = [along_dp(picked[step], step) for step in range(1, DP)]
    with jax.named_scope("layer_second"):
        updated_second, stats = layer(spot, arrays, pieces, weight, all_gains, stream, False)
        stats = gather_dp(stats)
    with jax.named_scope("hessian"):
        near = after([rows[0], rows[2]], [stats[0]])
        far = after([rows[1]], [near[0]] + stats[1:])
        rows = [picked[0], near[0], far[0], near[1]]
        rows += [shift(value, 0, 0, 1) for value in rows]
        row_gain = lax.dynamic_slice_in_dim(all_gains, quarter * (TENSOR // DP), TENSOR // DP, 0)
        hessian = gram(spot, rows, cols, stats, row_gain, gain[None, :])
    sections = jnp.where(first, updated_first, updated_second)
    return (hessian[None], sections.reshape(1, M, TOK, WIDTH))


def solution(mesh):
    return jax.shard_map(
        body,
        mesh=mesh,
        in_specs=(
            P(None, "dp", "tensor"),
            P("pipe", "tensor"),
            P("pipe", "tensor", None, None),
            P("pipe", "tensor", None),
        ),
        out_specs=(P("pipe", "dp", "tensor"), P("pipe", None, "dp", "tensor")),
        check_vma=False,
    )
```

time: 220 us -> 194 us (0.88)
  waiting for transfers between devices: 58.5 us -> 34.3 us
  Pallas kernels: 80.8 us -> 60.8 us
  starting transfers between devices: 46 us -> 62.1 us
    all_gather x3 -> x2, waiting for transfers between devices: 44.5 us -> 10.3 us  [the longest x1 10.3 us: body(): gathered = lax.all_gather(own, 'tensor', axis=0, tiled=True)]
    ppermute x7 -> x29, starting transfers between devices: 33.3 us -> 50.1 us  [the longest x23 42.3 us: shift(): return lax.ppermute(value, 'tensor', pairs)]
    pallas_call x1, Pallas kernels: 28.8 us -> 13.8 us  [build_dense(): pl.pallas_call(build_kernel, grid_spec=pltpu.PrefetchScalarGridSpec(num_s...]
    ppermute x7 -> x29, waiting for transfers between devices: 4.59 us -> 14.8 us  [the longest x23 11.1 us: shift(): return lax.ppermute(value, 'tensor', pairs)]
    pallas_call x3 -> x6, Pallas kernels: 52 us -> 46.9 us  [the longest x2 29 us: layer(): pl.pallas_call(lambda *refs: layer_kernel(pieces, count, straight, *refs)...]
  transfers between devices with their start and end apart: 12 -> 33, of which waited for: 6 -> 9; matrix products, arithmetic and copies ran while one was open for 8% -> 10% of each run, Pallas kernels for 21% -> 17%
where the time goes in v2:
time: 194 us; the launch traced here: 193 us
  starting transfers between devices  62.1 us (32%)
  Pallas kernels  60.8 us (31%)
  waiting for transfers between devices  34.3 us (18%)
  local copies, waits for them, and re-layouts  18.7 us (10%)
  between operations  14.4 us (7%)
  other arithmetic  2.93 us (2%)
    ppermute x23, starting transfers between devices, shift(): return lax.ppermute(value, 'tensor', pairs)  42.3 us
    pallas_call x2, Pallas kernels, layer(): pl.pallas_call(lambda *refs: layer_kernel(pieces, count, straight, *refs)...  29 us
    pallas_call x1, Pallas kernels, build_dense(): pl.pallas_call(build_kernel, grid_spec=pltpu.PrefetchScalarGridSpec(num_s...  13.8 us
    squeeze x1, local copies, waits for them, and re-layouts, build_dense(): blocks = values.reshape(WIDTH // BLOCK, KEEP, BLOCK, BLOCK)  13.8 us
    pallas_call x1, Pallas kernels, gram(): pl.pallas_call(gram_kernel, in_specs=[SMEM] + [ANY] * (2 * DP) + [VMEM] *...  13.6 us
    ppermute x23, waiting for transfers between devices, shift(): return lax.ppermute(value, 'tensor', pairs)  11.1 us
    all_gather x1, waiting for transfers between devices, body(): gathered = lax.all_gather(own, 'tensor', axis=0, tiled=True)  10.3 us
    ppermute x1, waiting for transfers between devices, body(): received = lax.ppermute(updated_first, 'pipe', [(0, 1)])  8.51 us
  transfers between devices with their start and end apart: 33, of which 9 were waited for; matrix products, arithmetic and copies ran while one was open for 10% of the time, Pallas kernels for 17%

profile of v2, /device:TPU:1, one launch (start us, length us, event | category | flops | bytes accessed | tf_op | source)
XLA Modules:
  0.0 193.2 jit_solution(17282047637271140173)
XLA Ops:
  7.2 0.7 all-gather.4.cloned.1.call-update
  7.9 0.7 reduce
  8.6 0.6 broadcast_in_dim.13
  9.3 7.3 %all-to-all-start = ((f32[16,1,768]{2,1,0:T(1,128)}), f32[16,1,768]{2,1,0:T(1,128)S(1)}, u32[]{:S(2)}, u32[]{:S(2)}) async-start(f32[16,1,768]{2,1,0:T(1,128)} %broadcast_in_dim.13), calls=%async_computation | async-start | bytes 98304 | tf_op jit(solution)/shard_map/gains/all_to_all | solution.py:378
  16.7 0.6 pad_add_fusion.refs_0_.spot_ref
  17.3 13.8 %squeeze.7.blocks_ref = bf16[12,48,64,64]{3,2,1,0:T(8,128)(2,1)} reshape(bf16[1,12,48,4096]{3,2,1,0:T(8,128)(2,1)} %param.6) | data formatting | bytes 9437184 | tf_op jit(solution)/shard_map/weight/reshape;weight/squeeze | solution.py:47
  31.0 0.6 copy.11
  31.6 13.8 %build_dense.1.refs_1_ = bf16[3,12288,256]{2,1,0:T(8,128)(2,1)} custom-call(s32[12,48]{1,0:T(8,128)} %bitcast.18, bf16[12,48,64,64]{3,2,1,0:T(8,128)(2,1)} %squeeze.7.blocks_ref), custom_call_target="tpu_custom_call" | custom-call | bytes 33554432 | tf_op jit(solution)/shard_map/weight/build_dense/pallas_call | solution.py:49
  45.5 10.3 %all-gather.4.cloned.1.call-done.refs_4_ = bf16[4096,768]{1,0:T(8,128)(2,1)} async-done(((bf16[256,768]{1,0:T(8,128)(2,1)}), bf16[4096,768]{1,0:T(8,128)(2,1)}) %all-gather.4.cloned.1.call-update) | async-done | bytes 6291472 | tf_op jit(solution)/shard_map/rows_first/all_gather | solution.py:376
  55.8 14.4 %layer.2 = (bf16[256,768]{1,0:T(8,128)(2,1)}, f32[256,128]{1,0:T(8,128)}) custom-call(s32[4]{0:T(128)} %pad_add_fusion.refs_0_.spot_ref, bf16[3,12288,256]{2,1,0:T(8,128)(2,1)} %build_dense.1.refs_1_, f32[16,1,768]{2,1,0:T(1,128)} %copy-done.10, bf16[256,768]{1,0:T(8,128)(2,1)} %bitcast.16, bf16[4096,768]{1,0:T(8,128)(2,1)} %all-gather.4.cloned.1.call-done.refs_4_), custom_call_target="tpu_custom_call" | custom-call | flops 4831838208 | bytes 25165824 | tf_op jit(solution)/shard_map/layer_first/layer/pallas_call | solution.py:156
  70.2 4.6 %collective-permute-start = (bf16[256,768]{1,0:T(8,128)(2,1)}, bf16[256,768]{1,0:T(8,128)(2,1)S(1)}, u32[]{:S(2)}, u32[]{:S(2)}) collective-permute-start(bf16[256,768]{1,0:T(8,128)(2,1)} %get-tuple-element.11), channel_id=1, source_target_pairs={{0,16},{1,17},{2,18},{3,19},{4,20},{5,21},{6,22},{7,23},{8,24},{9,... | collective-permute-start | bytes 1179656 | tf_op jit(solution)/shard_map/hand_over/ppermute | solution.py:387
  74.8 8.5 %collective-permute-done = bf16[256,768]{1,0:T(8,128)(2,1)S(1)} collective-permute-done((bf16[256,768]{1,0:T(8,128)(2,1)}, bf16[256,768]{1,0:T(8,128)(2,1)S(1)}, u32[]{:S(2)}, u32[]{:S(2)}) %collective-permute-start) | collective-permute-done | bytes 393248 | tf_op jit(solution)/shard_map/hand_over/ppermute | solution.py:387
  83.3 0.8 select_add_fusion
  84.1 1.2 collective-permute-start.2
  85.8 1.5 collective-permute-start.1
  87.3 1.9 collective-permute-start.12
  89.2 5.7 %collective-permute-done.2.refs_4_.refs_7_ = bf16[256,768]{1,0:T(8,128)(2,1)S(1)} collective-permute-done((bf16[256,768]{1,0:T(8,128)(2,1)S(1)}, bf16[256,768]{1,0:T(8,128)(2,1)S(1)}, u32[]{:S(2)}, u32[]{:S(2)}) %collective-permute-start.2) | collective-permute-done | bytes 393248 | tf_op jit(solution)/shard_map/rows_second/ppermute | solution.py:342
  94.9 0.5 collective-permute-start.6
  95.4 2.7 %collective-permute-start.5 = (bf16[256,768]{1,0:T(8,128)(2,1)S(1)}, bf16[256,768]{1,0:T(8,128)(2,1)S(1)}, u32[]{:S(2)}, u32[]{:S(2)}) collective-permute-start(bf16[256,768]{1,0:T(8,128)(2,1)S(1)} %collective-permute-done.4.refs_5_.refs_8_), channel_id=1, source_target_pairs={{0,6},{1,7},{2,0},{3,1},{4,2},{5,3},{6,4},{7,5},{8,14},{9,15},{10,... | collective-permute-start | bytes 1179656 | tf_op jit(solution)/shard_map/rows_second/ppermute | solution.py:342
  98.1 2.9 %collective-permute-start.13 = (bf16[256,768]{1,0:T(8,128)(2,1)S(1)}, bf16[256,768]{1,0:T(8,128)(2,1)S(1)}, u32[]{:S(2)}, u32[]{:S(2)}) collective-permute-start(bf16[256,768]{1,0:T(8,128)(2,1)S(1)} %collective-permute-done.1.refs_2_.refs_5_), channel_id=1, source_target_pairs={{0,1},{1,0},{2,3},{3,2},{4,5},{5,4},{6,7},{7,6},{8,9},{9,8},{10,11... | collective-permute-start | bytes 1179656 | tf_op jit(solution)/shard_map/rows_second/ppermute | solution.py:342
  101.1 2.4 %collective-permute-done.6.refs_7_.refs_10_ = bf16[256,768]{1,0:T(8,128)(2,1)S(1)} collective-permute-done((bf16[256,768]{1,0:T(8,128)(2,1)S(1)}, bf16[256,768]{1,0:T(8,128)(2,1)S(1)}, u32[]{:S(2)}, u32[]{:S(2)}) %collective-permute-start.6) | collective-permute-done | bytes 393248 | tf_op jit(solution)/shard_map/rows_second/ppermute | solution.py:342
  103.5 2.9 %collective-permute-start.16 = (bf16[256,768]{1,0:T(8,128)(2,1)S(1)}, bf16[256,768]{1,0:T(8,128)(2,1)S(1)}, u32[]{:S(2)}, u32[]{:S(2)}) collective-permute-start(bf16[256,768]{1,0:T(8,128)(2,1)S(1)} %collective-permute-done.4.refs_5_.refs_8_), channel_id=1, source_target_pairs={{0,1},{1,0},{2,3},{3,2},{4,5},{5,4},{6,7},{7,6},{8,9},{9,8},{10,11... | collective-permute-start | bytes 1179656 | tf_op jit(solution)/shard_map/rows_second/ppermute | solution.py:342
  106.5 1.6 collective-permute-start.14
  108.2 2.9 %collective-permute-start.9 = (bf16[80,768]{1,0:T(8,128)(2,1)S(1)}, bf16[80,768]{1,0:T(8,128)(2,1)}, u32[]{:S(2)}, u32[]{:S(2)}) collective-permute-start(bf16[80,768]{1,0:T(8,128)(2,1)S(1)} %slice.14), channel_id=1, source_target_pairs={{0,6},{1,7},{2,0},{3,1},{4,2},{5,3},{6,4},{7,5},{8,14},{9,15},{10,... | collective-permute-start | bytes 368648 | tf_op jit(solution)/shard_map/rows_second/ppermute | solution.py:342
  111.2 1.1 collective-permute-start.7
  112.3 1.9 collective-permute-start.20
  114.2 0.5 collective-permute-start.21
  114.8 1.8 collective-permute-done.7.refs_8_.refs_11_
  116.5 1.0 collective-permute-start.18
  117.6 0.7 copy-done.20
  118.3 4.4 %pick.1 = (bf16[512,768]{1,0:T(8,128)(2,1)}, bf16[512,768]{1,0:T(8,128)(2,1)}, bf16[512,768]{1,0:T(8,128)(2,1)}, bf16[512,768]{1,0:T(8,128)(2,1)}) custom-call(s32[4]{0:T(128)} %pad_add_fusion.refs_0_.spot_ref, bf16[256,768]{1,0:T(8,128)(2,1)} %copy-done, bf16[256,768]{1,0:T(8,128)(2,1)} %copy-done.8, bf16[256,768]{1,0:T(8,128)(2,1)} %copy-done.3, ...), custom_call_target="tpu_custom_call" | custom-call | bytes 6291456 | tf_op jit(solution)/shard_map/hessian_rows/pick/pallas_call | solution.py:213
  122.7 1.3 collective-permute-start.10
  124.0 1.5 collective-permute-start.11
  125.5 1.5 collective-permute-start.22
  127.0 14.5 %layer.3 = (bf16[256,768]{1,0:T(8,128)(2,1)}, f32[256,128]{1,0:T(8,128)}) custom-call(s32[4]{0:T(128)} %pad_add_fusion.refs_0_.spot_ref, bf16[3,12288,256]{2,1,0:T(8,128)(2,1)} %build_dense.1.refs_1_, f32[16,1,768]{2,1,0:T(1,128)} %copy-done.10, bf16[256,768]{1,0:T(8,128)(2,1)} %copy-done, bf16[256,768]{1,0:T(8,128)(2,1)} %copy-done, ...), custom_call_target="tpu_custom_call" | custom-call | flops 4831838208 | bytes 25165824 | tf_op jit(solution)/shard_map/layer_second/layer/pallas_call | solution.py:156
  141.9 1.7 collective-permute-start.24
  143.7 1.5 collective-permute-start.25
  145.1 16.9 %collective-permute-start.26 = (bf16[512,768]{1,0:T(8,128)(2,1)}, bf16[512,768]{1,0:T(8,128)(2,1)}, u32[]{:S(2)}, u32[]{:S(2)}) collective-permute-start(bf16[512,768]{1,0:T(8,128)(2,1)} %get-tuple-element.12.refs_0_), channel_id=1, source_target_pairs={{0,1},{1,0},{2,3},{3,2},{4,5},{5,4},{6,7},{7,6},{8,9},{9,8},{10,11... | collective-permute-start | bytes 2359304 | tf_op jit(solution)/shard_map/hessian/ppermute | solution.py:342
  162.0 3.1 %collective-permute-done.23.refs_2_.refs_9_ = f32[256,128]{1,0:T(8,128)S(1)} collective-permute-done((f32[256,128]{1,0:T(8,128)}, f32[256,128]{1,0:T(8,128)S(1)}, u32[]{:S(2)}, u32[]{:S(2)}) %collective-permute-start.23) | collective-permute-done | bytes 131104 | tf_op jit(solution)/shard_map/layer_second/ppermute | solution.py:327
  165.1 0.6 collective-permute-start.27
  165.7 0.6 collective-permute-done.24.refs_3_.refs_10_
  166.4 0.6 copy-done.18
  167.0 1.3 collective-permute-start.28
  168.4 1.3 constant_dynamic-slice_fusion.refs_13_
  169.7 0.8 broadcast_select_fusion
  170.5 1.1 collective-permute-done.28.refs_6_
  171.8 0.7 copy-done.23
  172.7 13.6 %gram.1 = f32[3072,768]{1,0:T(8,128)} custom-call(s32[4]{0:T(128)} %pad_add_fusion.refs_0_.spot_ref, bf16[512,768]{1,0:T(8,128)(2,1)} %get-tuple-element.12.refs_0_, bf16[512,768]{1,0:T(8,128)(2,1)} %get-tuple-element.16.refs_1_, bf16[512,768]{1,0:T(8,128)(2,1)} %after.3.refs_2_, bf16[512,768]{1,0:T(8,128)(2,1)} %get-tuple-element.18.refs_3_, ...), custom_call_target="tpu_custom_call" | custom-call | flops 4831838208 | bytes 17301504 | tf_op jit(solution)/shard_map/hessian/gram/pallas_call | solution.py:303
  (86 shorter events, 1.9 us)
Async XLA Ops:
  7.2 23.9 %copy-start.21 = (s32[1,12,48]{2,0,1:T(1,128)S(1)}, s32[1,12,48]{2,0,1:T(1,128)}, u32[]{:S(2)}) copy-start(s32[1,12,48]{2,0,1:T(1,128)} %param.7) | copy-start | bytes 6916
  7.2 48.6 %all-gather.4.cloned.1.call-start = ((), (), s32[]{:S(2)}) async-start(), calls=%async_computation.1 | async-start | bytes 6684672 | tf_op jit(solution)/shard_map/rows_first/all_gather | solution.py:376
  9.3 36.2 %all-to-all-start = ((f32[16,1,768]{2,1,0:T(1,128)}), f32[16,1,768]{2,1,0:T(1,128)S(1)}, u32[]{:S(2)}, u32[]{:S(2)}) async-start(f32[16,1,768]{2,1,0:T(1,128)} %broadcast_in_dim.13), calls=%async_computation | async-start | bytes 98304 | tf_op jit(solution)/shard_map/gains/all_to_all | solution.py:378
  16.6 153.9 %all-gather.6.cloned.1.call-start = ((), (), s32[]{:S(2)}) async-start(), calls=%async_computation.2 | async-start | bytes 1966080 | tf_op jit(solution)/shard_map/columns/all_gather | solution.py:390
  45.5 37.8 %copy-start.1 = (bf16[4,64,768]{2,1,0:T(8,128)(2,1)S(1)}, bf16[4,64,768]{2,1,0:T(8,128)(2,1)}, u32[]{:S(2)}) copy-start(bf16[4,64,768]{2,1,0:T(8,128)(2,1)} %param.4) | copy-start | bytes 1179652
  45.5 10.3 %copy-start.10 = (f32[16,1,768]{2,1,0:T(1,128)}, f32[16,1,768]{2,1,0:T(1,128)S(1)}, u32[]{:S(2)}) copy-start(f32[16,1,768]{2,1,0:T(1,128)S(1)} %all-to-all-done.refs_2_) | copy-start | bytes 147460
  70.2 13.1 %collective-permute-start = (bf16[256,768]{1,0:T(8,128)(2,1)}, bf16[256,768]{1,0:T(8,128)(2,1)S(1)}, u32[]{:S(2)}, u32[]{:S(2)}) collective-permute-start(bf16[256,768]{1,0:T(8,128)(2,1)} %get-tuple-element.11), channel_id=1, source_target_pairs={{0,16},{1,17},{2,18},{3,19},{4,20},{5,21},{6,22},{7,23},{8,24},{9,... | collective-permute-start | bytes 1179656 | tf_op jit(solution)/shard_map/hand_over/ppermute | solution.py:387
  84.1 34.1 %copy-start = (bf16[256,768]{1,0:T(8,128)(2,1)}, bf16[256,768]{1,0:T(8,128)(2,1)S(1)}, u32[]{:S(2)}) copy-start(bf16[256,768]{1,0:T(8,128)(2,1)S(1)} %get-tuple-element.21.refs_1_.refs_3_.refs_4_) | copy-start | bytes 1179652
  84.1 10.7 %collective-permute-start.2 = (bf16[256,768]{1,0:T(8,128)(2,1)S(1)}, bf16[256,768]{1,0:T(8,128)(2,1)S(1)}, u32[]{:S(2)}, u32[]{:S(2)}) collective-permute-start(bf16[256,768]{1,0:T(8,128)(2,1)S(1)} %get-tuple-element.21.refs_1_.refs_3_.refs_4_), channel_id=1, source_target_pairs={{0,2},{1,3},{2,4},{3,5},{4,6},{5,7},{6,0},{7,1},{8,10},{9,11},{10,... | collective-permute-start | bytes 1179656 | tf_op jit(solution)/shard_map/rows_second/ppermute | solution.py:342
  85.3 10.0 %collective-permute-start.4 = (bf16[256,768]{1,0:T(8,128)(2,1)S(1)}, bf16[256,768]{1,0:T(8,128)(2,1)S(1)}, u32[]{:S(2)}, u32[]{:S(2)}) collective-permute-start(bf16[256,768]{1,0:T(8,128)(2,1)S(1)} %get-tuple-element.21.refs_1_.refs_3_.refs_4_), channel_id=1, source_target_pairs={{0,8},{1,9},{2,10},{3,11},{4,12},{5,13},{6,14},{7,15},{8,0},{9,1},... | collective-permute-start | bytes 1179656 | tf_op jit(solution)/shard_map/rows_second/ppermute | solution.py:342
  85.8 12.3 %collective-permute-start.1 = (bf16[256,768]{1,0:T(8,128)(2,1)S(1)}, bf16[256,768]{1,0:T(8,128)(2,1)S(1)}, u32[]{:S(2)}, u32[]{:S(2)}) collective-permute-start(bf16[256,768]{1,0:T(8,128)(2,1)S(1)} %get-tuple-element.21.refs_1_.refs_3_.refs_4_), channel_id=1, source_target_pairs={{0,6},{1,7},{2,0},{3,1},{4,2},{5,3},{6,4},{7,5},{8,14},{9,15},{10,... | collective-permute-start | bytes 1179656 | tf_op jit(solution)/shard_map/rows_second/ppermute | solution.py:342
  87.3 13.7 %collective-permute-start.12 = (bf16[256,768]{1,0:T(8,128)(2,1)S(1)}, bf16[256,768]{1,0:T(8,128)(2,1)S(1)}, u32[]{:S(2)}, u32[]{:S(2)}) collective-permute-start(bf16[256,768]{1,0:T(8,128)(2,1)S(1)} %get-tuple-element.21.refs_1_.refs_3_.refs_4_), channel_id=1, source_target_pairs={{0,1},{1,0},{2,3},{3,2},{4,5},{5,4},{6,7},{7,6},{8,9},{9,8},{10,11... | collective-permute-start | bytes 1179656 | tf_op jit(solution)/shard_map/rows_second/ppermute | solution.py:342
  94.9 23.4 %copy-start.6 = (bf16[256,768]{1,0:T(8,128)(2,1)}, bf16[256,768]{1,0:T(8,128)(2,1)S(1)}, u32[]{:S(2)}) copy-start(bf16[256,768]{1,0:T(8,128)(2,1)S(1)} %collective-permute-done.2.refs_4_.refs_7_) | copy-start | bytes 1179652
  94.9 8.6 %collective-permute-start.6 = (bf16[256,768]{1,0:T(8,128)(2,1)S(1)}, bf16[256,768]{1,0:T(8,128)(2,1)S(1)}, u32[]{:S(2)}, u32[]{:S(2)}) collective-permute-start(bf16[256,768]{1,0:T(8,128)(2,1)S(1)} %collective-permute-done.2.refs_4_.refs_7_), channel_id=1, source_target_pairs={{0,8},{1,9},{2,10},{3,11},{4,12},{5,13},{6,14},{7,15},{8,0},{9,1},... | collective-permute-start | bytes 1179656 | tf_op jit(solution)/shard_map/rows_second/ppermute | solution.py:342
  95.4 11.1 %collective-permute-start.3 = (bf16[256,768]{1,0:T(8,128)(2,1)S(1)}, bf16[256,768]{1,0:T(8,128)(2,1)S(1)}, u32[]{:S(2)}, u32[]{:S(2)}) collective-permute-start(bf16[256,768]{1,0:T(8,128)(2,1)S(1)} %collective-permute-done.2.refs_4_.refs_7_), channel_id=1, source_target_pairs={{0,2},{1,3},{2,4},{3,5},{4,6},{5,7},{6,0},{7,1},{8,10},{9,11},{10,... | collective-permute-start | bytes 1179656 | tf_op jit(solution)/shard_map/rows_second/ppermute | solution.py:342
  95.4 22.9 %copy-start.7 = (bf16[256,768]{1,0:T(8,128)(2,1)}, bf16[256,768]{1,0:T(8,128)(2,1)S(1)}, u32[]{:S(2)}) copy-start(bf16[256,768]{1,0:T(8,128)(2,1)S(1)} %collective-permute-done.4.refs_5_.refs_8_) | copy-start | bytes 1179652
  95.4 11.2 %collective-permute-start.5 = (bf16[256,768]{1,0:T(8,128)(2,1)S(1)}, bf16[256,768]{1,0:T(8,128)(2,1)S(1)}, u32[]{:S(2)}, u32[]{:S(2)}) collective-permute-start(bf16[256,768]{1,0:T(8,128)(2,1)S(1)} %collective-permute-done.4.refs_5_.refs_8_), channel_id=1, source_target_pairs={{0,6},{1,7},{2,0},{3,1},{4,2},{5,3},{6,4},{7,5},{8,14},{9,15},{10,... | collective-permute-start | bytes 1179656 | tf_op jit(solution)/shard_map/rows_second/ppermute | solution.py:342
  98.1 20.2 %copy-start.8 = (bf16[256,768]{1,0:T(8,128)(2,1)}, bf16[256,768]{1,0:T(8,128)(2,1)S(1)}, u32[]{:S(2)}) copy-start(bf16[256,768]{1,0:T(8,128)(2,1)S(1)} %collective-permute-done.1.refs_2_.refs_5_) | copy-start | bytes 1179652
  98.1 10.1 %collective-permute-start.13 = (bf16[256,768]{1,0:T(8,128)(2,1)S(1)}, bf16[256,768]{1,0:T(8,128)(2,1)S(1)}, u32[]{:S(2)}, u32[]{:S(2)}) collective-permute-start(bf16[256,768]{1,0:T(8,128)(2,1)S(1)} %collective-permute-done.1.refs_2_.refs_5_), channel_id=1, source_target_pairs={{0,1},{1,0},{2,3},{3,2},{4,5},{5,4},{6,7},{7,6},{8,9},{9,8},{10,11... | collective-permute-start | bytes 1179656 | tf_op jit(solution)/shard_map/rows_second/ppermute | solution.py:342
  101.0 16.5 %copy-start.13 = (bf16[256,768]{1,0:T(8,128)(2,1)}, bf16[256,768]{1,0:T(8,128)(2,1)S(1)}, u32[]{:S(2)}) copy-start(bf16[256,768]{1,0:T(8,128)(2,1)S(1)} %collective-permute-done.12.refs_14_) | copy-start | bytes 1179652
  101.0 10.2 %collective-permute-start.15 = (bf16[256,768]{1,0:T(8,128)(2,1)S(1)}, bf16[256,768]{1,0:T(8,128)(2,1)S(1)}, u32[]{:S(2)}, u32[]{:S(2)}) collective-permute-start(bf16[256,768]{1,0:T(8,128)(2,1)S(1)} %collective-permute-done.2.refs_4_.refs_7_), channel_id=1, source_target_pairs={{0,1},{1,0},{2,3},{3,2},{4,5},{5,4},{6,7},{7,6},{8,9},{9,8},{10,11... | collective-permute-start | bytes 1179656 | tf_op jit(solution)/shard_map/rows_second/ppermute | solution.py:342
  103.5 14.8 %copy-start.4 = (bf16[256,768]{1,0:T(8,128)(2,1)}, bf16[256,768]{1,0:T(8,128)(2,1)S(1)}, u32[]{:S(2)}) copy-start(bf16[256,768]{1,0:T(8,128)(2,1)S(1)} %collective-permute-done.6.refs_7_.refs_10_) | copy-start | bytes 1179652
  103.5 11.2 %collective-permute-start.16 = (bf16[256,768]{1,0:T(8,128)(2,1)S(1)}, bf16[256,768]{1,0:T(8,128)(2,1)S(1)}, u32[]{:S(2)}, u32[]{:S(2)}) collective-permute-start(bf16[256,768]{1,0:T(8,128)(2,1)S(1)} %collective-permute-done.4.refs_5_.refs_8_), channel_id=1, source_target_pairs={{0,1},{1,0},{2,3},{3,2},{4,5},{5,4},{6,7},{7,6},{8,9},{9,8},{10,11... | collective-permute-start | bytes 1179656 | tf_op jit(solution)/shard_map/rows_second/ppermute | solution.py:342
  106.4 11.8 %copy-start.3 = (bf16[256,768]{1,0:T(8,128)(2,1)}, bf16[256,768]{1,0:T(8,128)(2,1)S(1)}, u32[]{:S(2)}) copy-start(bf16[256,768]{1,0:T(8,128)(2,1)S(1)} %collective-permute-done.3.refs_3_.refs_6_) | copy-start | bytes 1179652
  106.4 5.8 %collective-permute-start.8 = (bf16[80,768]{1,0:T(8,128)(2,1)S(1)}, bf16[80,768]{1,0:T(8,128)(2,1)S(1)}, u32[]{:S(2)}, u32[]{:S(2)}) collective-permute-start(bf16[80,768]{1,0:T(8,128)(2,1)S(1)} %slice.13), channel_id=1, source_target_pairs={{0,2},{1,3},{2,4},{3,5},{4,6},{5,7},{6,0},{7,1},{8,10},{9,11},{10,... | collective-permute-start | bytes 368648 | tf_op jit(solution)/shard_map/rows_second/ppermute | solution.py:342
  106.5 11.8 %copy-start.5 = (bf16[256,768]{1,0:T(8,128)(2,1)}, bf16[256,768]{1,0:T(8,128)(2,1)S(1)}, u32[]{:S(2)}) copy-start(bf16[256,768]{1,0:T(8,128)(2,1)S(1)} %collective-permute-done.5.refs_6_.refs_9_) | copy-start | bytes 1179652
  106.5 18.9 %collective-permute-start.14 = (bf16[256,768]{1,0:T(8,128)(2,1)S(1)}, bf16[256,768]{1,0:T(8,128)(2,1)}, u32[]{:S(2)}, u32[]{:S(2)}) collective-permute-start(bf16[256,768]{1,0:T(8,128)(2,1)S(1)} %collective-permute-done.3.refs_3_.refs_6_), channel_id=1, source_target_pairs={{0,1},{1,0},{2,3},{3,2},{4,5},{5,4},{6,7},{7,6},{8,9},{9,8},{10,11... | collective-permute-start | bytes 1179656 | tf_op jit(solution)/shard_map/rows_second/ppermute | solution.py:342
  108.2 9.3 %copy-start.14 = (bf16[256,768]{1,0:T(8,128)(2,1)}, bf16[256,768]{1,0:T(8,128)(2,1)S(1)}, u32[]{:S(2)}) copy-start(bf16[256,768]{1,0:T(8,128)(2,1)S(1)} %collective-permute-done.13.refs_15_) | copy-start | bytes 1179652
  108.2 6.0 %collective-permute-start.9 = (bf16[80,768]{1,0:T(8,128)(2,1)S(1)}, bf16[80,768]{1,0:T(8,128)(2,1)}, u32[]{:S(2)}, u32[]{:S(2)}) collective-permute-start(bf16[80,768]{1,0:T(8,128)(2,1)S(1)} %slice.14), channel_id=1, source_target_pairs={{0,6},{1,7},{2,0},{3,1},{4,2},{5,3},{6,4},{7,5},{8,14},{9,15},{10,... | collective-permute-start | bytes 368648 | tf_op jit(solution)/shard_map/rows_second/ppermute | solution.py:342
  111.2 6.4 %copy-start.15 = (bf16[256,768]{1,0:T(8,128)(2,1)}, bf16[256,768]{1,0:T(8,128)(2,1)S(1)}, u32[]{:S(2)}) copy-start(bf16[256,768]{1,0:T(8,128)(2,1)S(1)} %collective-permute-done.15.refs_17_) | copy-start | bytes 1179652
  111.2 5.3 %collective-permute-start.7 = (bf16[96,768]{1,0:T(8,128)(2,1)S(1)}, bf16[96,768]{1,0:T(8,128)(2,1)S(1)}, u32[]{:S(2)}, u32[]{:S(2)}) collective-permute-start(bf16[96,768]{1,0:T(8,128)(2,1)S(1)} %slice.12), channel_id=1, source_target_pairs={{0,8},{1,9},{2,10},{3,11},{4,12},{5,13},{6,14},{7,15},{8,0},{9,1},... | collective-permute-start | bytes 442376 | tf_op jit(solution)/shard_map/rows_second/ppermute | solution.py:342
  112.3 5.3 %collective-permute-start.20 = (bf16[80,768]{1,0:T(8,128)(2,1)S(1)}, bf16[80,768]{1,0:T(8,128)(2,1)S(1)}, u32[]{:S(2)}, u32[]{:S(2)}) collective-permute-start(bf16[80,768]{1,0:T(8,128)(2,1)S(1)} %collective-permute-done.8.refs_9_.refs_12_), channel_id=1, source_target_pairs={{0,1},{1,0},{2,3},{3,2},{4,5},{5,4},{6,7},{7,6},{8,9},{9,8},{10,11... | collective-permute-start | bytes 368648 | tf_op jit(solution)/shard_map/rows_second/ppermute | solution.py:342
  114.2 8.5 %collective-permute-start.21 = (bf16[80,768]{1,0:T(8,128)(2,1)}, bf16[80,768]{1,0:T(8,128)(2,1)}, u32[]{:S(2)}, u32[]{:S(2)}) collective-permute-start(bf16[80,768]{1,0:T(8,128)(2,1)} %collective-permute-done.9.refs_10_.refs_13_), channel_id=1, source_target_pairs={{0,1},{1,0},{2,3},{3,2},{4,5},{5,4},{6,7},{7,6},{8,9},{9,8},{10,11... | collective-permute-start | bytes 368648 | tf_op jit(solution)/shard_map/rows_second/ppermute | solution.py:342
  114.7 12.3 %collective-permute-start.17 = (bf16[256,768]{1,0:T(8,128)(2,1)S(1)}, bf16[256,768]{1,0:T(8,128)(2,1)}, u32[]{:S(2)}, u32[]{:S(2)}) collective-permute-start(bf16[256,768]{1,0:T(8,128)(2,1)S(1)} %collective-permute-done.5.refs_6_.refs_9_), channel_id=1, source_target_pairs={{0,1},{1,0},{2,3},{3,2},{4,5},{5,4},{6,7},{7,6},{8,9},{9,8},{10,11... | collective-permute-start | bytes 1179656 | tf_op jit(solution)/shard_map/rows_second/ppermute | solution.py:342
  116.5 10.4 %collective-permute-start.18 = (bf16[256,768]{1,0:T(8,128)(2,1)S(1)}, bf16[256,768]{1,0:T(8,128)(2,1)}, u32[]{:S(2)}, u32[]{:S(2)}) collective-permute-start(bf16[256,768]{1,0:T(8,128)(2,1)S(1)} %collective-permute-done.6.refs_7_.refs_10_), channel_id=1, source_target_pairs={{0,1},{1,0},{2,3},{3,2},{4,5},{5,4},{6,7},{7,6},{8,9},{9,8},{10,11... | collective-permute-start | bytes 1179656 | tf_op jit(solution)/shard_map/rows_second/ppermute | solution.py:342
  118.2 5.7 %collective-permute-start.19 = (bf16[96,768]{1,0:T(8,128)(2,1)S(1)}, bf16[96,768]{1,0:T(8,128)(2,1)}, u32[]{:S(2)}, u32[]{:S(2)}) collective-permute-start(bf16[96,768]{1,0:T(8,128)(2,1)S(1)} %collective-permute-done.7.refs_8_.refs_11_), channel_id=1, source_target_pairs={{0,1},{1,0},{2,3},{3,2},{4,5},{5,4},{6,7},{7,6},{8,9},{9,8},{10,11... | collective-permute-start | bytes 442376 | tf_op jit(solution)/shard_map/rows_second/ppermute | solution.py:342
  122.7 21.0 %collective-permute-start.10 = (bf16[512,768]{1,0:T(8,128)(2,1)}, bf16[512,768]{1,0:T(8,128)(2,1)S(1)}, u32[]{:S(2)}, u32[]{:S(2)}) collective-permute-start(bf16[512,768]{1,0:T(8,128)(2,1)} %get-tuple-element.13), channel_id=1, source_target_pairs={{0,32},{32,64},{64,96},{96,0},{1,33},{33,65},{65,97},{97,1},{2,34}... | collective-permute-start | bytes 2359304 | tf_op jit(solution)/shard_map/hessian_rows/ppermute | solution.py:327
  124.0 21.2 %collective-permute-start.11 = (bf16[512,768]{1,0:T(8,128)(2,1)}, bf16[512,768]{1,0:T(8,128)(2,1)}, u32[]{:S(2)}, u32[]{:S(2)}) collective-permute-start(bf16[512,768]{1,0:T(8,128)(2,1)} %get-tuple-element.14), channel_id=1, source_target_pairs={{0,96},{32,0},{64,32},{96,64},{1,97},{33,1},{65,33},{97,65},{2,98}... | collective-permute-start | bytes 2359304 | tf_op jit(solution)/shard_map/hessian_rows/ppermute | solution.py:327
  125.5 44.2 %copy-start.12 = (bf16[256,768]{1,0:T(8,128)(2,1)S(1)}, bf16[256,768]{1,0:T(8,128)(2,1)}, u32[]{:S(2)}) copy-start(bf16[256,768]{1,0:T(8,128)(2,1)} %get-tuple-element.11) | copy-start | bytes 1179652
  125.5 40.9 %collective-permute-start.22 = (bf16[512,768]{1,0:T(8,128)(2,1)}, bf16[512,768]{1,0:T(8,128)(2,1)}, u32[]{:S(2)}, u32[]{:S(2)}) collective-permute-start(bf16[512,768]{1,0:T(8,128)(2,1)} %get-tuple-element.17), channel_id=1, source_target_pairs={{0,64},{32,96},{64,0},{96,32},{1,65},{33,97},{65,1},{97,33},{2,66}... | collective-permute-start | bytes 2359304 | tf_op jit(solution)/shard_map/hessian_rows/ppermute | solution.py:327
  141.5 23.6 %collective-permute-start.23 = (f32[256,128]{1,0:T(8,128)}, f32[256,128]{1,0:T(8,128)S(1)}, u32[]{:S(2)}, u32[]{:S(2)}) collective-permute-start(f32[256,128]{1,0:T(8,128)} %get-tuple-element.15.refs_2_.refs_8_), channel_id=1, source_target_pairs={{0,32},{32,64},{64,96},{96,0},{1,33},{33,65},{65,97},{97,1},{2,34}... | collective-permute-start | bytes 393224 | tf_op jit(solution)/shard_map/layer_second/ppermute | solution.py:327
  141.9 24.4 %collective-permute-start.24 = (f32[256,128]{1,0:T(8,128)}, f32[256,128]{1,0:T(8,128)S(1)}, u32[]{:S(2)}, u32[]{:S(2)}) collective-permute-start(f32[256,128]{1,0:T(8,128)} %get-tuple-element.15.refs_2_.refs_8_), channel_id=1, source_target_pairs={{0,64},{32,96},{64,0},{96,32},{1,65},{33,97},{65,1},{97,33},{2,66}... | collective-permute-start | bytes 393224 | tf_op jit(solution)/shard_map/layer_second/ppermute | solution.py:327
  143.7 18.4 %copy-start.2 = (bf16[512,768]{1,0:T(8,128)(2,1)}, bf16[512,768]{1,0:T(8,128)(2,1)S(1)}, u32[]{:S(2)}) copy-start(bf16[512,768]{1,0:T(8,128)(2,1)S(1)} %collective-permute-done.10.refs_0_) | copy-start | bytes 2359300
  143.7 22.7 %collective-permute-start.25 = (f32[256,128]{1,0:T(8,128)}, f32[256,128]{1,0:T(8,128)S(1)}, u32[]{:S(2)}, u32[]{:S(2)}) collective-permute-start(f32[256,128]{1,0:T(8,128)} %get-tuple-element.15.refs_2_.refs_8_), channel_id=1, source_target_pairs={{0,96},{32,0},{64,32},{96,64},{1,97},{33,1},{65,33},{97,65},{2,98}... | collective-permute-start | bytes 393224 | tf_op jit(solution)/shard_map/layer_second/ppermute | solution.py:327
  145.1 25.4 %collective-permute-start.26 = (bf16[512,768]{1,0:T(8,128)(2,1)}, bf16[512,768]{1,0:T(8,128)(2,1)}, u32[]{:S(2)}, u32[]{:S(2)}) collective-permute-start(bf16[512,768]{1,0:T(8,128)(2,1)} %get-tuple-element.12.refs_0_), channel_id=1, source_target_pairs={{0,1},{1,0},{2,3},{3,2},{4,5},{5,4},{6,7},{7,6},{8,9},{9,8},{10,11... | collective-permute-start | bytes 2359304 | tf_op jit(solution)/shard_map/hessian/ppermute | solution.py:342
  165.1 6.5 %collective-permute-start.27 = (bf16[512,768]{1,0:T(8,128)(2,1)}, bf16[512,768]{1,0:T(8,128)(2,1)S(1)}, u32[]{:S(2)}, u32[]{:S(2)}) collective-permute-start(bf16[512,768]{1,0:T(8,128)(2,1)} %get-tuple-element.16.refs_1_), channel_id=1, source_target_pairs={{0,1},{1,0},{2,3},{3,2},{4,5},{5,4},{6,7},{7,6},{8,9},{9,8},{10,11... | collective-permute-start | bytes 2359304 | tf_op jit(solution)/shard_map/hessian/ppermute | solution.py:342
  167.0 4.5 %collective-permute-start.28 = (bf16[512,768]{1,0:T(8,128)(2,1)}, bf16[512,768]{1,0:T(8,128)(2,1)S(1)}, u32[]{:S(2)}, u32[]{:S(2)}) collective-permute-start(bf16[512,768]{1,0:T(8,128)(2,1)} %after.3.refs_2_), channel_id=1, source_target_pairs={{0,1},{1,0},{2,3},{3,2},{4,5},{5,4},{6,7},{7,6},{8,9},{9,8},{10,11... | collective-permute-start | bytes 2359304 | tf_op jit(solution)/shard_map/hessian/ppermute | solution.py:342
  168.4 3.4 %collective-permute-start.29 = (bf16[512,768]{1,0:T(8,128)(2,1)}, bf16[512,768]{1,0:T(8,128)(2,1)}, u32[]{:S(2)}, u32[]{:S(2)}) collective-permute-start(bf16[512,768]{1,0:T(8,128)(2,1)} %get-tuple-element.18.refs_3_), channel_id=1, source_target_pairs={{0,1},{1,0},{2,3},{3,2},{4,5},{5,4},{6,7},{7,6},{8,9},{9,8},{10,11... | collective-permute-start | bytes 2359304 | tf_op jit(solution)/shard_map/hessian/ppermute | solution.py:342
  (9 other events, 16.0 us)
Sparse Core Ops, SparseCore 0:
  9.7 46.0 all-gather.3
  98.2 28.7 all-gather.5
